TPU v7x, 128 devices: a whole 4x4x4 slice. The times are simulated.
128 devices in a mesh: dp: 8 (over x, core), param: 16 (over z, y).
Axes of the slice: x: 4, y: 4, z: 4, core: 2. Of those that a mesh axis runs over, the one named last changes fastest.
Arguments:
- activations: bfloat16 [48, 2048, 8192], P('dp', None, 'param'), may hold values from -6 to 6
- output_gradient_rows: bfloat16 [48, 2048, 8192], P('dp', None, 'param'), may hold values from -0.19921875 to 0.19921875
- lengths: int32 [48], P('dp'), may hold values from 512 to 2048, as said below
- shrinking_factor: bfloat16 [8192, 128], P('param', 'dp'), may hold values from -0.0625 to 0.0625
- expanding_factor: bfloat16 [128, 8192], P('dp', 'param'), may hold values from -0.0625 to 0.0625
- shrinking_running_average: float32 [8192, 128], P('param', 'dp'), may hold values from -0.6 to 0.6
- shrinking_running_variance: float32 [8192, 128], P('param', 'dp'), may hold values from 0.01 to 1
- expanding_running_average: float32 [128, 8192], P('dp', 'param'), may hold values from -0.6 to 0.6
- expanding_running_variance: float32 [128, 8192], P('dp', 'param'), may hold values from 0.01 to 1
- up_rank_projector: float32 [128, 64], replicated
- up_width_projector: float32 [8192, 64], P('param'), may hold values from -0.0625 to 0.0625
- down_width_projector: float32 [8192, 64], P('param'), may hold values from -0.0625 to 0.0625
- down_rank_projector: float32 [128, 64], replicated
Outputs:
- features: float32 [48, 8192], P('dp', 'param')
Inputs may be any that keep to these rules, and one draw needn't show every extreme that they name: `lengths`: some example has 2048 valid tokens and some has 512.
All inputs are finite; a program needn't handle non-finite values.
Results may differ from a plain program's by a relative error of at most 0.00045.
Values may be sent and summed in bfloat16 or wider, within the bound.
No kernel may reach another device: no remote copies, remote signals or barrier semaphores. Data moves between devices by JAX's collectives and lax.ppermute only.
A program may use at most 128 MiB of HBM per device.

v0:
```python
import jax
import jax.numpy as jnp
from jax import lax
from jax.sharding import PartitionSpec as P


def precondition(grad, first, second):
    top = 0.9 * first + 0.1 * grad
    return top / (jnp.sqrt(0.999 * second + 0.001 * grad * grad) + 1e-08)


def body(
    activations,
    output_gradient_rows,
    lengths,
    shrinking_factor,
    expanding_factor,
    shrinking_running_average,
    shrinking_running_variance,
    expanding_running_average,
    expanding_running_variance,
    up_rank_projector,
    up_width_projector,
    down_width_projector,
    down_rank_projector,
):
    high = lax.Precision.HIGHEST
    down_rows, up_cols = (
        lax.all_gather(shrinking_factor, "dp", axis=1, tiled=True),
        lax.all_gather(expanding_factor, "dp", axis=0, tiled=True),
    )
    low_part = jnp.einsum("etd,dr->etr", activations, down_rows, preferred_element_type=jnp.float32)
    rise_part = jnp.einsum(
        "etd,rd->etr", output_gradient_rows, up_cols, preferred_element_type=jnp.float32
    )
    low_sum, rise_sum = lax.psum((low_part, rise_part), "param")
    positions = jnp.arange(low_sum.shape[1], dtype=jnp.int32)
    valid_mask = (positions[None, :] < lengths[:, None])[:, :, None]
    lowered_program = jnp.where(valid_mask, low_sum, 0.0).astype(jnp.bfloat16)
    raised_error = jnp.where(valid_mask, rise_sum, 0.0).astype(jnp.bfloat16)
    first_d, second_d, first_u, second_u = (
        lax.all_gather(shrinking_running_average, "dp", axis=1, tiled=True),
        lax.all_gather(shrinking_running_variance, "dp", axis=1, tiled=True),
        lax.all_gather(expanding_running_average, "dp", axis=0, tiled=True),
        lax.all_gather(expanding_running_variance, "dp", axis=0, tiled=True),
    )
    grad_up = jnp.einsum(
        "etr,etd->erd", lowered_program, output_gradient_rows, preferred_element_type=jnp.float32
    )
    grad_down = jnp.einsum(
        "etd,etr->edr", activations, raised_error, preferred_element_type=jnp.float32
    )
    pre_up = precondition(grad_up, first_u[None], second_u[None])
    pre_down = precondition(grad_down, first_d[None], second_d[None])
    width_up = jnp.einsum("erd,dj->erj", pre_up, up_width_projector, precision=high)
    part_up = jnp.einsum("ri,erj->eij", up_rank_projector, width_up, precision=high)
    width_down = jnp.einsum("edr,di->eri", pre_down, down_width_projector, precision=high)
    part_down = jnp.einsum("rj,eri->eji", down_rank_projector, width_down, precision=high)
    examples = part_up.shape[0]
    partial_value = jnp.concatenate(
        [part_up.reshape(examples, -1), part_down.reshape(examples, -1)], axis=1
    )
    total_width = partial_value.shape[1]
    share = total_width // lax.axis_size("param")
    summed = lax.psum(partial_value, "param")
    scale = lax.rsqrt(jnp.mean(summed * summed, axis=1) + 1e-06)
    owned = lax.dynamic_slice_in_dim(summed, lax.axis_index("param") * share, share, 1)
    return owned * scale[:, None]


def solution(mesh):
    in_specs = (
        P("dp", None, "param"),
        P("dp", None, "param"),
        P("dp"),
        P("param", "dp"),
        P("dp", "param"),
        P("param", "dp"),
        P("param", "dp"),
        P("dp", "param"),
        P("dp", "param"),
        P(),
        P("param", None),
        P("param", None),
        P(),
    )
    out_specs = P("dp", "param")
    return jax.shard_map(body, mesh=mesh, in_specs=in_specs, out_specs=out_specs, check_vma=False)
```

profile of v0, /device:TPU:6, one launch (start us, length us, event | category | flops | bytes accessed | tf_op | source)
XLA Modules:
  0.0 495.3 jit_solution(117838183500526161)
XLA Ops:
  6.5 13.1 %all_gather.22 = bf16[128,512]{1,0:T(8,128)(2,1)S(1)} all-gather(bf16[16,512]{1,0:T(8,128)(2,1)} %param.17), channel_id=1, replica_groups=mesh['dp'=8,'param'=16] {'dp'}, dimensions={0}, use_global_device_ids=true | all-gather | bytes 147456 | tf_op jit(solution)/shard_map/all_gather | solution.py:30
  19.6 11.5 %fusion.30 = f32[6,2048,128]{1,2,0:T(8,128)} fusion(bf16[6,2048,512]{2,1,0:T(8,128)(2,1)} %param.14, bf16[128,512]{1,0:T(8,128)(2,1)S(1)} %all_gather.22), kind=kOutput, calls=%fused_computation.37 | convolution fusion | flops 1610612736 | bytes 19005440 | tf_op jit(solution)/shard_map/etd,rd->etr/dot_general | solution.py:33
  31.1 12.7 %all_gather.19 = bf16[512,128]{0,1:T(8,128)(2,1)S(1)} all-gather(bf16[512,16]{0,1:T(8,128)(2,1)S(1)} %copy-done.8), channel_id=1, replica_groups=mesh['dp'=8,'param'=16] {'dp'}, dimensions={1}, use_global_device_ids=true | all-gather | bytes 147456 | tf_op jit(solution)/shard_map/all_gather | solution.py:29
  43.9 6.8 %fusion.33 = f32[6,2048,128]{1,2,0:T(8,128)} fusion(bf16[6,2048,512]{2,1,0:T(8,128)(2,1)S(1)} %copy-done.1, bf16[512,128]{0,1:T(8,128)(2,1)S(1)} %all_gather.19), kind=kOutput, calls=%fused_computation.40 | convolution fusion | flops 1610612736 | bytes 19005440 | tf_op jit(solution)/shard_map/etd,dr->etr/dot_general | solution.py:32
  50.7 0.1 iota_compare_fusion
  50.8 12.8 %all_gather.23 = f32[512,128]{0,1:T(8,128)S(1)} all-gather(f32[512,16]{0,1:T(8,128)S(1)} %copy-done.2), channel_id=1, replica_groups=mesh['dp'=8,'param'=16] {'dp'}, dimensions={1}, use_global_device_ids=true | all-gather | bytes 294912 | tf_op jit(solution)/shard_map/all_gather | solution.py:43
  63.6 12.8 %all_gather.21 = f32[512,128]{0,1:T(8,128)S(1)} all-gather(f32[512,16]{0,1:T(8,128)S(1)} %copy-done.3), channel_id=1, replica_groups=mesh['dp'=8,'param'=16] {'dp'}, dimensions={1}, use_global_device_ids=true | all-gather | bytes 294912 | tf_op jit(solution)/shard_map/all_gather | solution.py:42
  76.5 278.5 %all-reduce.5 = (bf16[6,2048,128]{1,2,0:T(8,128)(2,1)}, bf16[6,2048,128]{1,2,0:T(8,128)(2,1)}) all-reduce(f32[6,2048,128]{1,2,0:T(8,128)} %fusion.30, f32[6,2048,128]{1,2,0:T(8,128)} %fusion.33), channel_id=1, replica_groups=mesh['dp'=8,'param'=16] {'param'}, use_global_device_ids=true, to_apply=%region_1.0 | all-reduce | flops 3145728 | bytes 18874368 | tf_op jit(solution)/shard_map/psum | solution.py:36
  355.0 7.3 %fusion.1 = f32[6,128,512]{2,1,0:T(8,128)S(1)} fusion(bf16[6,2048,512]{2,1,0:T(8,128)(2,1)} %param.13, bf16[6,2048,128]{1,2,0:T(8,128)(2,1)} %get-tuple-element.5, pred[6,2048]{1,0:T(8,128)(4,1)S(1)} %iota_compare_fusion), kind=kOutput, calls=%fused_computation.3 | convolution fusion | flops 1612185600 | bytes 17313792 | tf_op jit(solution)/shard_map/etd,etr->edr/dot_general | solution.py:50
  362.3 2.2 fusion.15
  364.6 0.3 convolution_bitcast_fusion
  364.9 0.1 copy.15
  365.0 0.1 reshape.41
  365.1 7.3 %fusion = f32[6,128,512]{2,1,0:T(8,128)S(1)} fusion(bf16[6,2048,512]{2,1,0:T(8,128)(2,1)} %param.14, bf16[6,2048,128]{1,2,0:T(8,128)(2,1)} %get-tuple-element.6, pred[6,2048]{1,0:T(8,128)(4,1)S(1)} %iota_compare_fusion), kind=kOutput, calls=%fused_computation.2 | convolution fusion | flops 1612185600 | bytes 17313792 | tf_op jit(solution)/shard_map/etr,etd->erd/dot_general | solution.py:47
  372.5 13.0 %all_gather.20 = f32[128,512]{1,0:T(8,128)S(1)} all-gather(f32[16,512]{1,0:T(8,128)S(1)} %copy-done.4), channel_id=1, replica_groups=mesh['dp'=8,'param'=16] {'dp'}, dimensions={0}, use_global_device_ids=true | all-gather | bytes 294912 | tf_op jit(solution)/shard_map/all_gather | solution.py:45
  385.5 12.8 %all_gather.18 = f32[128,512]{1,0:T(8,128)S(1)} all-gather(f32[16,512]{1,0:T(8,128)S(1)} %copy-done.5), channel_id=1, replica_groups=mesh['dp'=8,'param'=16] {'dp'}, dimensions={0}, use_global_device_ids=true | all-gather | bytes 294912 | tf_op jit(solution)/shard_map/all_gather | solution.py:44
  398.4 2.2 fusion.17
  400.6 0.3 convolution_bitcast_fusion.1
  401.0 0.1 copy.14
  401.1 0.1 reshape.40
  401.2 0.7 pad_maximum_fusion
  401.9 84.0 %all-reduce.4.cloned.1.call-done = f32[6,8192]{1,0:T(8,128)} async-done(((f32[6,8192]{1,0:T(8,128)}), f32[6,8192]{1,0:T(8,128)}) %all-reduce.4.cloned.1.call-update) | async-done | bytes 196624 | tf_op jit(solution)/shard_map/psum | solution.py:65
  486.0 1.1 multiply_reduce_fusion
  487.1 1.4 dynamic-slice_multiply_fusion
  (29 shorter events, 0.2 us)
Async XLA Ops:
  6.5 355.8 %copy-start = (f32[512,64]{0,1:T(8,128)S(1)}, f32[512,64]{0,1:T(8,128)}, u32[]{:S(2)}) copy-start(f32[512,64]{0,1:T(8,128)} %param.24) | copy-start | bytes 393220
  6.5 479.4 %all-reduce.4.cloned.1.call-start = ((), (), s32[]{:S(2)}) async-start(), calls=%async_computation | async-start | bytes 524288 | tf_op jit(solution)/shard_map/psum | solution.py:65
  19.6 11.5 %copy-start.8 = (bf16[512,16]{0,1:T(8,128)(2,1)S(1)}, bf16[512,16]{0,1:T(8,128)(2,1)}, u32[]{:S(2)}) copy-start(bf16[512,16]{0,1:T(8,128)(2,1)} %param.16) | copy-start | bytes 49156
  19.6 24.3 %copy-start.1 = (bf16[6,2048,512]{2,1,0:T(8,128)(2,1)S(1)}, bf16[6,2048,512]{2,1,0:T(8,128)(2,1)}, u32[]{:S(2)}) copy-start(bf16[6,2048,512]{2,1,0:T(8,128)(2,1)} %param.13) | copy-start | bytes 37748740
  43.9 6.8 %copy-start.9 = (s32[6]{0:T(128)S(1)}, s32[6]{0:T(128)}, u32[]{:S(2)}) copy-start(s32[6]{0:T(128)} %param.15) | copy-start | bytes 76
  43.9 6.9 %copy-start.2 = (f32[512,16]{0,1:T(8,128)S(1)}, f32[512,16]{0,1:T(8,128)}, u32[]{:S(2)}) copy-start(f32[512,16]{0,1:T(8,128)} %param.19) | copy-start | bytes 98308
  43.9 19.8 %copy-start.3 = (f32[512,16]{0,1:T(8,128)S(1)}, f32[512,16]{0,1:T(8,128)}, u32[]{:S(2)}) copy-start(f32[512,16]{0,1:T(8,128)} %param.18) | copy-start | bytes 98308
  362.3 2.2 copy-start.6
  365.1 7.4 %copy-start.4 = (f32[16,512]{1,0:T(8,128)S(1)}, f32[16,512]{1,0:T(8,128)}, u32[]{:S(2)}) copy-start(f32[16,512]{1,0:T(8,128)} %param.21) | copy-start | bytes 98308
  365.1 20.4 %copy-start.5 = (f32[16,512]{1,0:T(8,128)S(1)}, f32[16,512]{1,0:T(8,128)}, u32[]{:S(2)}) copy-start(f32[16,512]{1,0:T(8,128)} %param.20) | copy-start | bytes 98308
  372.5 25.9 %copy-start.10 = (f32[512,64]{0,1:T(8,128)S(1)}, f32[512,64]{0,1:T(8,128)}, u32[]{:S(2)}) copy-start(f32[512,64]{0,1:T(8,128)} %param.23) | copy-start | bytes 393220
  398.4 2.2 copy-start.7
Sparse Core Ops, SparseCore 0:
  402.0 83.8 all-reduce.3
where the time goes:
time: 496 us; the launch traced here: 495 us
  blocking collectives  356 us (72%)
  waiting for transfers between devices  84 us (17%)
  matrix products  38 us (8%)
  between operations  13.6 us (3%)
    psum x1, blocking collectives, body(): low_sum, rise_sum = lax.psum((low_part, rise_part), 'param')  278 us
    psum x1, waiting for transfers between devices, body(): summed = lax.psum(partial_value, 'param')  84 us
    all_gather x1, blocking collectives, body(): lax.all_gather(expanding_factor, 'dp', axis=0, tiled=True)  13.1 us
    all_gather x1, blocking collectives, body(): lax.all_gather(expanding_running_variance, 'dp', axis=0, tiled=True)  13 us
    all_gather x1, blocking collectives, body(): lax.all_gather(shrinking_running_variance, 'dp', axis=1, tiled=True)  12.8 us
    all_gather x1, blocking collectives, body(): lax.all_gather(expanding_running_average, 'dp', axis=0, tiled=True)  12.8 us
    all_gather x1, blocking collectives, body(): lax.all_gather(shrinking_running_average, 'dp', axis=1, tiled=True)  12.8 us
    all_gather x1, blocking collectives, body(): lax.all_gather(shrinking_factor, 'dp', axis=1, tiled=True)  12.7 us
  transfers between devices with their start and end apart: 1, of which 1 were waited for; matrix products, arithmetic and copies ran while one was open for 0% of the time, Pallas kernels for 0%

commit v1 on v0

v1 whole, which is shorter than its diff:
```python
import functools

import jax
import jax.numpy as jnp
from jax import lax
from jax.experimental import pallas as pl
from jax.experimental.pallas import tpu as pltpu
from jax.sharding import Mesh, PartitionSpec as P

BLK = 128
FOOT = 16
RES = 128.0
TOP = 32767.0
MIB = 1024 * 1024
VMEM = pltpu.VMEM
SMEM = pltpu.SMEM
F32 = jnp.float32
BF16 = jnp.bfloat16
I16 = jnp.int16
I32 = jnp.int32


def scale_code(peak):
    return jnp.ceil(jnp.log(jnp.maximum(peak, 1e-30)) * (RES / 0.6931471805599453)) + 1.0


def scale_of(code):
    return jnp.exp2(code * (1.0 / RES))


def encode(x):
    code = scale_code(jnp.max(jnp.abs(x), axis=0, keepdims=True))
    q = jnp.round(x * (TOP / scale_of(code)))
    return q.astype(I32).astype(I16), code


def partial_kernel(nblk, tab, base, w, a_hbm, g_hbm, q, abuf, gbuf, codes, sems):
    first = base[0]

    def copies(k):
        e, t = tab[0, first + k], pl.multiple_of(tab[1, first + k], BLK)
        return (
            pltpu.make_async_copy(a_hbm.at[e, pl.ds(t, BLK)], abuf.at[k], sems.at[0, k]),
            pltpu.make_async_copy(g_hbm.at[e, pl.ds(t, BLK)], gbuf.at[k], sems.at[1, k]),
        )

    for k in range(nblk):
        for c in copies(k):
            c.start()
    rank = w.shape[1] // 2
    ws = w[:, :rank, :].reshape(-1, w.shape[2])
    we = w[:, rank:, :].reshape(-1, w.shape[2])
    codes[...] = jnp.zeros_like(codes)
    nt = (((1,), (1,)), ((), ()))
    for k in range(nblk):
        for c in copies(k):
            c.wait()
        live = lax.broadcasted_iota(I32, (BLK, 1), 0) < tab[2, first + k]
        for i, (buf, weight) in enumerate(((abuf, ws), (gbuf, we))):
            x = lax.dot_general(buf[k], weight, nt, preferred_element_type=F32)
            x = jnp.where(live, x, 0.0)
            coded, code = encode(x)
            q[k * BLK : (k + 1) * BLK, i * 128 : (i + 1) * 128] = coded
            codes[k : k + 1, i * 128 : (i + 1) * 128] = code
    q[nblk * BLK :, :] = codes[...].astype(I32).astype(I16)


def partial_piece(tab, base, w, a, g, nblk):
    rows = nblk * BLK
    return pl.pallas_call(
        functools.partial(partial_kernel, nblk),
        out_shape=jax.ShapeDtypeStruct((rows + FOOT, 256), I16),
        in_specs=[
            pl.BlockSpec(memory_space=SMEM),
            pl.BlockSpec(memory_space=SMEM),
            pl.BlockSpec(memory_space=VMEM),
            pl.BlockSpec(memory_space=pl.ANY),
            pl.BlockSpec(memory_space=pl.ANY),
        ],
        out_specs=pl.BlockSpec(memory_space=VMEM),
        scratch_shapes=[
            VMEM((nblk, BLK, 512), BF16),
            VMEM((nblk, BLK, 512), BF16),
            VMEM((FOOT, 256), F32),
            pltpu.SemaphoreType.DMA((2, nblk)),
        ],
        compiler_params=pltpu.CompilerParams(vmem_limit_bytes=16 * MIB),
        cost_estimate=pl.CostEstimate(
            flops=4 * rows * 512 * 128, bytes_accessed=rows * (2048 + 512), transcendentals=0
        ),
    )(tab, base, w, a, g)


def scales_of(refs, rows, count):
    return [scale_of(r[rows:, :].astype(I32).astype(F32)) * (1.0 / TOP) for r in refs]


def value(ref, start, n):
    return ref[pl.ds(start, n), :].astype(I32).astype(F32)


def middle_kernel(rows, sub, step, order, q0, q1, q2, q3, r0, r1, r2, r3, scales, codes):
    refs, outs = (q0, q1, q2, q3), (r0, r1, r2, r3)
    for i, s in enumerate(scales_of(refs, rows, rows // BLK)):
        scales[i] = s
    for s in range(4):
        codes[...] = jnp.zeros_like(codes)
        begin = order[s] * sub
        for j in range(sub // step):
            at = pl.multiple_of(begin + j * step, step)
            blk = at // BLK
            total = None
            for i, r in enumerate(refs):
                v = value(r, at, step) * scales[i, pl.ds(blk, 1), :]
                total = v if total is None else total + v
            coded, code = encode(total)
            outs[s][j * step : (j + 1) * step, :] = coded
            codes[j : j + 1, :] = code
        outs[s][sub:, :] = codes[...].astype(I32).astype(I16)


def middle_sum(order, pieces, rows, sub, step):
    return pl.pallas_call(
        functools.partial(middle_kernel, rows, sub, step),
        out_shape=[jax.ShapeDtypeStruct((sub + FOOT, 256), I16)] * 4,
        in_specs=[pl.BlockSpec(memory_space=SMEM)] + [pl.BlockSpec(memory_space=VMEM)] * 4,
        out_specs=[pl.BlockSpec(memory_space=VMEM)] * 4,
        scratch_shapes=[VMEM((4, FOOT, 256), F32), VMEM((FOOT, 256), F32)],
        compiler_params=pltpu.CompilerParams(vmem_limit_bytes=16 * MIB),
        cost_estimate=pl.CostEstimate(
            flops=rows * 256 * 8, bytes_accessed=rows * 256 * 10, transcendentals=0
        ),
    )(order, *pieces)


def last_kernel(sub, step, r0, r1, r2, r3, out):
    refs = (r0, r1, r2, r3)
    scales = scales_of(refs, sub, sub // step)
    for j in range(sub // step):
        total = None
        for i, r in enumerate(refs):
            v = value(r, j * step, step) * scales[i][j : j + 1, :]
            total = v if total is None else total + v
        out[j * step : (j + 1) * step, :] = total.astype(BF16)


def last_sum(pieces, sub, step):
    return pl.pallas_call(
        functools.partial(last_kernel, sub, step),
        out_shape=jax.ShapeDtypeStruct((sub, 256), BF16),
        in_specs=[pl.BlockSpec(memory_space=VMEM)] * 4,
        out_specs=pl.BlockSpec(memory_space=VMEM),
        compiler_params=pltpu.CompilerParams(vmem_limit_bytes=8 * MIB),
        cost_estimate=pl.CostEstimate(
            flops=sub * 256 * 8, bytes_accessed=sub * 256 * 10, transcendentals=0
        ),
    )(*pieces)


def precondition(grad, first, second):
    top = 0.9 * first + 0.1 * grad
    return top / (jnp.sqrt(0.999 * second + 0.001 * grad * grad) + 1e-08)


def grads_kernel(nb, sub, tab, heads, place, *refs):
    pieces = refs[:8]
    a_hbm, g_hbm, moments, urp, uwp, dwp, drp, out, lr, abuf, gbuf, up, down, sems, lsems = refs[8:]

    def copies(b):
        e, t = tab[0, b], pl.multiple_of(tab[1, b], BLK)
        return (
            pltpu.make_async_copy(a_hbm.at[e, pl.ds(t, BLK)], abuf.at[b], sems.at[0, b]),
            pltpu.make_async_copy(g_hbm.at[e, pl.ds(t, BLK)], gbuf.at[b], sems.at[1, b]),
        )

    spread = []
    for p, piece in enumerate(pieces):
        for s in range(4):
            at = pl.multiple_of(place[p * 4 + s] * sub, 32)
            spread.append(
                pltpu.make_async_copy(
                    piece.at[pl.ds(s * sub, sub)], lr.at[pl.ds(at, sub)], lsems.at[p * 4 + s]
                )
            )
    for c in spread:
        c.start()

    def begin(b, carry):
        for c in copies(b):
            c.start()
        return carry

    total = heads[6]
    lax.fori_loop(0, total, begin, 0)
    for c in spread:
        c.wait()
    tn = (((0,), (0,)), ((), ()))
    high = lax.Precision.HIGHEST
    rank = moments.shape[1] // 4

    def moment(i):
        return moments[:, i * rank : (i + 1) * rank, :].reshape(-1, moments.shape[2])

    for e in range(6):
        up[...] = jnp.zeros_like(up)
        down[...] = jnp.zeros_like(down)

        def step(b, carry):
            for c in copies(b):
                c.wait()
            rows = pl.ds(pl.multiple_of(b * BLK, BLK), BLK)
            up[...] += lax.dot_general(lr[rows, :128], gbuf[b], tn, preferred_element_type=F32)
            down[...] += lax.dot_general(lr[rows, 128:], abuf[b], tn, preferred_element_type=F32)
            return carry

        lax.fori_loop(heads[e], heads[e + 1], step, 0)
        for i, (grad, width, side) in enumerate(((up, uwp, urp), (down, dwp, drp))):
            pre = precondition(grad[...], moment(2 * i), moment(2 * i + 1))
            wide = jnp.dot(pre, width[...], precision=high, preferred_element_type=F32)
            if i == 0:
                part = lax.dot_general(side[...], wide, tn, precision=high, preferred_element_type=F32)
            else:
                part = lax.dot_general(side[...], wide, tn, precision=high, preferred_element_type=F32)
            out[e, i * 64 : (i + 1) * 64, :] = part


def grads(tab, heads, place, pieces, a, g, moments, urp, uwp, dwp, drp, nb, sub):
    return pl.pallas_call(
        functools.partial(grads_kernel, nb, sub),
        out_shape=jax.ShapeDtypeStruct((6, 128, 64), F32),
        in_specs=[pl.BlockSpec(memory_space=SMEM)] * 3
        + [pl.BlockSpec(memory_space=pl.ANY)] * 10
        + [pl.BlockSpec(memory_space=VMEM)] * 5,
        out_specs=pl.BlockSpec(memory_space=VMEM),
        scratch_shapes=[
            VMEM((nb * BLK, 256), BF16),
            VMEM((nb, BLK, 512), BF16),
            VMEM((nb, BLK, 512), BF16),
            VMEM((128, 512), F32),
            VMEM((128, 512), F32),
            pltpu.SemaphoreType.DMA((2, nb)),
            pltpu.SemaphoreType.DMA((32,)),
        ],
        compiler_params=pltpu.CompilerParams(vmem_limit_bytes=48 * MIB),
        cost_estimate=pl.CostEstimate(
            flops=4 * nb * BLK * 512 * 128, bytes_accessed=nb * BLK * 2560, transcendentals=0
        ),
    )(tab, heads, place, *pieces, a, g, moments, urp, uwp, dwp, drp)


def block_table(lengths, nb):
    counts = (lengths + (BLK - 1)) // BLK
    ends = jnp.cumsum(counts)
    heads = jnp.concatenate([jnp.zeros((1,), I32), ends]).astype(I32)
    b = jnp.arange(nb, dtype=I32)
    e = jnp.sum((b[:, None] >= ends[None, :]).astype(I32), axis=1)
    inside = e < lengths.shape[0]
    e = jnp.minimum(e, lengths.shape[0] - 1)
    pick = (e[:, None] == jnp.arange(lengths.shape[0], dtype=I32)[None, :]).astype(I32)
    t = jnp.where(inside, (b - jnp.sum(pick * heads[None, :-1], axis=1)) * BLK, 0)
    rows = jnp.where(inside, jnp.clip(jnp.sum(pick * lengths[None, :], axis=1) - t, 0, BLK), 0)
    return jnp.stack([e, t, rows]).astype(I32), heads


def shift_of(n, s):
    return [(i, (i + s) % n) for i in range(n)]


def features(nb, lengths, w, moments, a, g, urp, uwp, dwp, drp):
    tokens = nb * BLK
    rows, sub, step, per = tokens // 8, tokens // 32, 32, nb // 8
    tab, heads = block_table(lengths, nb)
    here = {"y": lax.axis_index("y").astype(I32), "z": lax.axis_index("z").astype(I32)}
    halves = (("y", "z"), ("z", "y"))

    def send(x, axis, s):
        return lax.ppermute(x, axis, shift_of(4, s))

    coded = {}
    for s in (2, 1, 3, 0):
        for h, (first, _) in enumerate(halves):
            base = h * (nb // 2) + ((here[first] + s) % 4) * per
            coded[h, s] = partial_piece(tab, base.reshape(1), w, a, g, per)
    got = {(h, s): coded[h, s] if s == 0 else send(coded[h, s], halves[h][0], s) for h, s in coded}
    shifts = jnp.arange(4, dtype=I32)
    mids = [
        middle_sum((here[second] + shifts) % 4, [got[h, s] for s in range(4)], rows, sub, step)
        for h, (_, second) in enumerate(halves)
    ]
    sums = []
    for h, (_, second) in enumerate(halves):
        arrived = [mids[h][s] if s == 0 else send(mids[h][s], second, s) for s in range(4)]
        sums.append(last_sum(arrived, sub, step))
    pieces, place = [], []
    for h, (first, second) in enumerate(halves):
        block = jnp.concatenate(
            [sums[h] if s == 0 else send(sums[h], second, s) for s in range(4)], axis=0
        )
        for s in range(4):
            pieces.append(block if s == 0 else send(block, first, s))
            owner = (here[first] - s) % 4
            place.append(h * 16 + owner * 4 + (here[second] - shifts) % 4)
    place = jnp.concatenate(place).astype(I32)
    return grads(tab, heads, place, pieces, a, g, moments, urp, uwp, dwp, drp, nb, sub)


def body(a, g, lengths, sf, ef, sra, srv, era, erv, urp, uwp, dwp, drp):
    dp, param = ("x", "core"), ("z", "y")
    w = lax.all_gather(jnp.concatenate([sf.T, ef], axis=0), dp, axis=0)
    moments = lax.all_gather(jnp.concatenate([era, erv, sra.T, srv.T], axis=0), dp, axis=0)
    nb = a.shape[0] * a.shape[1] // BLK
    part = features(nb, lengths, w, moments, a, g, urp, uwp, dwp, drp)
    owned = jnp.swapaxes(part.reshape(6, 16, 8, 64), 0, 1)
    raw = jnp.sum(lax.all_to_all(owned, param, 0, 0, tiled=True), axis=0)
    square = lax.psum(lax.psum(jnp.sum(raw * raw, axis=(1, 2)), "y"), "z")
    scale = lax.rsqrt(square / 8192.0 + 1e-06)
    return (raw * scale[:, None, None]).reshape(6, 512)


def solution(mesh):
    grid = Mesh(mesh.devices.reshape(4, 2, 4, 4), ("x", "core", "z", "y"))
    dp, param = ("x", "core"), ("z", "y")
    in_specs = (
        P(dp, None, param),
        P(dp, None, param),
        P(dp),
        P(param, dp),
        P(dp, param),
        P(param, dp),
        P(param, dp),
        P(dp, param),
        P(dp, param),
        P(),
        P(param, None),
        P(param, None),
        P(),
    )
    return jax.shard_map(body, mesh=grid, in_specs=in_specs, out_specs=P(dp, param), check_vma=False)
```

time: 496 us -> 347 us (0.70)
  blocking collectives: 356 us -> 44.7 us
  Pallas kernels: 0 us -> 107 us
  local copies, waits for them, and re-layouts: 0.49 us -> 77 us
  matrix products: 38 us -> 0 us
  starting transfers between devices: 0.01 us -> 35.7 us
  waiting for transfers between devices: 84 us -> 58.2 us
    psum x1 -> x2, blocking collectives: 278 us -> 17.4 us  [body(): square = lax.psum(lax.psum(jnp.sum(raw * raw, axis=(1, 2)), 'y'), 'z')]
    pallas_call x0 -> x13, Pallas kernels: none -> 107 us  [the longest x8 71.2 us: partial_piece(): pl.pallas_call(functools.partial(partial_kernel, nblk), out_shape=jax.Sha...]
    psum x1 -> x0, waiting for transfers between devices: 84 us -> none  [body(): summed = lax.psum(partial_value, 'param')]
    unnamed x22 -> x66, local copies, waits for them, and re-layouts: 0.05 us -> 76.4 us
    all_gather x6 -> x1, blocking collectives: 77.3 us -> 12.8 us  [body(): w = lax.all_gather(jnp.concatenate([sf.T, ef], axis=0), dp, axis=0)]
    ppermute x0 -> x24, waiting for transfers between devices: none -> 58.2 us  [send(): return lax.ppermute(x, axis, shift_of(4, s))]
    dot_general x8 -> x0, matrix products: 38 us -> none  [the longest x1 11.5 us: body(): jnp.einsum('etd,rd->etr', output_gradient_rows, up_cols, preferred_elemen...]
    ppermute x0 -> x24, starting transfers between devices: none -> 35.7 us  [send(): return lax.ppermute(x, axis, shift_of(4, s))]
  transfers between devices with their start and end apart: 1 -> 25, of which waited for: 1 -> 10; matrix products, arithmetic and copies ran while one was open for 0% -> 1% of each run, Pallas kernels for 0% -> 19%
where the time goes in v1:
time: 347 us; the launch traced here: 343 us
  Pallas kernels  107 us (31%)
  local copies, waits for them, and re-layouts  77 us (22%)
  waiting for transfers between devices  58.2 us (17%)
  blocking collectives  44.7 us (13%)
  starting transfers between devices  35.7 us (10%)
  between operations  13.8 us (4%)
  other arithmetic  6.57 us (2%)
    unnamed x66, local copies, waits for them, and re-layouts  76.4 us
    pallas_call x8, Pallas kernels, partial_piece(): pl.pallas_call(functools.partial(partial_kernel, nblk), out_shape=jax.Sha...  71.2 us
    ppermute x24, waiting for transfers between devices, send(): return lax.ppermute(x, axis, shift_of(4, s))  58.2 us
    ppermute x24, starting transfers between devices, send(): return lax.ppermute(x, axis, shift_of(4, s))  35.7 us
    pallas_call x1, Pallas kernels, grads(): pl.pallas_call(functools.partial(grads_kernel, nb, sub), out_shape=jax.Sh...  30.4 us
    psum x2, blocking collectives, body(): square = lax.psum(lax.psum(jnp.sum(raw * raw, axis=(1, 2)), 'y'), 'z')  17.4 us
    all_to_all x1, blocking collectives, body(): raw = jnp.sum(lax.all_to_all(owned, param, 0, 0, tiled=True), axis=0)  14.5 us
    all_gather x1, blocking collectives, body(): w = lax.all_gather(jnp.concatenate([sf.T, ef], axis=0), dp, axis=0)  12.8 us
  transfers between devices with their start and end apart: 25, of which 10 were waited for; matrix products, arithmetic and copies ran while one was open for 1% of the time, Pallas kernels for 19%

profile of v1, /device:TPU:6, one launch (start us, length us, event | category | flops | bytes accessed | tf_op | source)
XLA Modules:
  0.0 342.9 jit_solution(15060302291356534803)
XLA Ops:
  8.3 12.8 %all-gather = bf16[256,512]{1,0:T(8,128)(2,1)S(1)} all-gather(bf16[32,512]{1,0:T(8,128)(2,1)S(1)} %pad_maximum_fusion.3), channel_id=2, replica_groups=mesh['x'=4,'core'=2,'z'=4,'y'=4] {'x','core'}, dimensions={0}, use_global_device_ids=true | all-gather | bytes 294912 | tf_op jit(solution)/shard_map/all_gather | solution.py:309
  26.5 4.6 %copy-done.8 = bf16[6,2048,512]{2,1,0:T(8,128)(2,1)S(1)} copy-done((bf16[6,2048,512]{2,1,0:T(8,128)(2,1)S(1)}, bf16[6,2048,512]{2,1,0:T(8,128)(2,1)}, u32[]{:S(2)}) %copy-start.8) | copy-done | bytes 12582936
  31.0 8.3 %shard_map.134 = s16[1552,256]{1,0:T(8,128)(2,1)S(1)} custom-call(s32[3,96]{1,0:T(4,128)S(1)} %pad_add_fusion.tab, s32[1]{0:T(128)} %bitcast.13.base, bf16[8,32,512]{2,1,0:T(8,128)(2,1)S(1)} %bitcast.43, bf16[6,2048,512]{2,1,0:T(8,128)(2,1)S(1)} %copy-done, bf16[6,2048,512]{2,1,0:T(8,128)(2,1)S(1)} %copy-done.8), custom_call_target="tpu_custom_call" | custom-call | flops 402653184 | bytes 3932160 | tf_op jit(solution)/shard_map/pallas_call | solution.py:70
  41.4 4.6 %copy-done.1 = bf16[6,2048,512]{2,1,0:T(8,128)(2,1)S(1)} copy-done((bf16[6,2048,512]{2,1,0:T(8,128)(2,1)S(1)}, bf16[6,2048,512]{2,1,0:T(8,128)(2,1)}, u32[]{:S(2)}) %copy-start.1) | copy-done | bytes 12582936
  46.0 4.6 %copy-done.9 = bf16[6,2048,512]{2,1,0:T(8,128)(2,1)S(1)} copy-done((bf16[6,2048,512]{2,1,0:T(8,128)(2,1)S(1)}, bf16[6,2048,512]{2,1,0:T(8,128)(2,1)}, u32[]{:S(2)}) %copy-start.9) | copy-done | bytes 12582936
  50.5 9.2 %shard_map.135 = s16[1552,256]{1,0:T(8,128)(2,1)} custom-call(s32[3,96]{1,0:T(4,128)S(1)} %pad_add_fusion.tab, s32[1]{0:T(128)} %bitcast.14.base, bf16[8,32,512]{2,1,0:T(8,128)(2,1)S(1)} %bitcast.44, bf16[6,2048,512]{2,1,0:T(8,128)(2,1)S(1)} %copy-done.1, bf16[6,2048,512]{2,1,0:T(8,128)(2,1)S(1)} %copy-done.9), custom_call_target="tpu_custom_call" | custom-call | flops 402653184 | bytes 3932160 | tf_op jit(solution)/shard_map/pallas_call | solution.py:70
  63.5 4.6 %copy-done.2 = bf16[6,2048,512]{2,1,0:T(8,128)(2,1)S(1)} copy-done((bf16[6,2048,512]{2,1,0:T(8,128)(2,1)S(1)}, bf16[6,2048,512]{2,1,0:T(8,128)(2,1)}, u32[]{:S(2)}) %copy-start.2) | copy-done | bytes 12582936
  68.0 4.6 %copy-done.10 = bf16[6,2048,512]{2,1,0:T(8,128)(2,1)S(1)} copy-done((bf16[6,2048,512]{2,1,0:T(8,128)(2,1)S(1)}, bf16[6,2048,512]{2,1,0:T(8,128)(2,1)}, u32[]{:S(2)}) %copy-start.10) | copy-done | bytes 12582936
  72.6 9.2 %shard_map.136 = s16[1552,256]{1,0:T(8,128)(2,1)} custom-call(s32[3,96]{1,0:T(4,128)S(1)} %pad_add_fusion.tab, s32[1]{0:T(128)} %bitcast.15.base, bf16[8,32,512]{2,1,0:T(8,128)(2,1)S(1)} %bitcast.45, bf16[6,2048,512]{2,1,0:T(8,128)(2,1)S(1)} %copy-done.2, bf16[6,2048,512]{2,1,0:T(8,128)(2,1)S(1)} %copy-done.10), custom_call_target="tpu_custom_call" | custom-call | flops 402653184 | bytes 3932160 | tf_op jit(solution)/shard_map/pallas_call | solution.py:70
  92.1 8.4 %shard_map.133.q0 = s16[1552,256]{1,0:T(8,128)(2,1)S(1)} custom-call(s32[3,96]{1,0:T(4,128)S(1)} %pad_add_fusion.tab, s32[1]{0:T(128)} %bitcast.12.base, bf16[8,32,512]{2,1,0:T(8,128)(2,1)S(1)} %bitcast.46, bf16[6,2048,512]{2,1,0:T(8,128)(2,1)S(1)} %copy-done.3, bf16[6,2048,512]{2,1,0:T(8,128)(2,1)S(1)} %copy-done.11), custom_call_target="tpu_custom_call" | custom-call | flops 402653184 | bytes 3932160 | tf_op jit(solution)/shard_map/pallas_call | solution.py:70
  119.7 9.2 %shard_map.128 = s16[1552,256]{1,0:T(8,128)(2,1)} custom-call(s32[3,96]{1,0:T(4,128)S(1)} %pad_add_fusion.tab, s32[1]{0:T(128)} %bitcast.9.base, bf16[8,32,512]{2,1,0:T(8,128)(2,1)S(1)} %bitcast.47, bf16[6,2048,512]{2,1,0:T(8,128)(2,1)S(1)} %copy-done.4, bf16[6,2048,512]{2,1,0:T(8,128)(2,1)S(1)} %copy-done.12), custom_call_target="tpu_custom_call" | custom-call | flops 402653184 | bytes 3932160 | tf_op jit(solution)/shard_map/pallas_call | solution.py:70
  138.9 9.2 %shard_map.129 = s16[1552,256]{1,0:T(8,128)(2,1)} custom-call(s32[3,96]{1,0:T(4,128)S(1)} %pad_add_fusion.tab, s32[1]{0:T(128)} %bitcast.10.base, bf16[8,32,512]{2,1,0:T(8,128)(2,1)S(1)} %bitcast.48, bf16[6,2048,512]{2,1,0:T(8,128)(2,1)S(1)} %copy-done.5, bf16[6,2048,512]{2,1,0:T(8,128)(2,1)S(1)} %copy-done.13), custom_call_target="tpu_custom_call" | custom-call | flops 402653184 | bytes 3932160 | tf_op jit(solution)/shard_map/pallas_call | solution.py:70
  149.0 4.6 %copy-done.6 = bf16[6,2048,512]{2,1,0:T(8,128)(2,1)S(1)} copy-done((bf16[6,2048,512]{2,1,0:T(8,128)(2,1)S(1)}, bf16[6,2048,512]{2,1,0:T(8,128)(2,1)}, u32[]{:S(2)}) %copy-start.6) | copy-done | bytes 12582936
  158.1 9.2 %shard_map.130 = s16[1552,256]{1,0:T(8,128)(2,1)} custom-call(s32[3,96]{1,0:T(4,128)S(1)} %pad_add_fusion.tab, s32[1]{0:T(128)} %bitcast.11.base, bf16[8,32,512]{2,1,0:T(8,128)(2,1)S(1)} %bitcast.49, bf16[6,2048,512]{2,1,0:T(8,128)(2,1)S(1)} %copy-done.6, bf16[6,2048,512]{2,1,0:T(8,128)(2,1)S(1)} %copy-done.14), custom_call_target="tpu_custom_call" | custom-call | flops 402653184 | bytes 3932160 | tf_op jit(solution)/shard_map/pallas_call | solution.py:70
  173.1 7.1 %collective-permute-done.18 = bf16[384,256]{1,0:T(8,128)(2,1)S(1)} collective-permute-done((bf16[384,256]{1,0:T(8,128)(2,1)}, bf16[384,256]{1,0:T(8,128)(2,1)S(1)}, u32[]{:S(2)}, u32[]{:S(2)}) %collective-permute-start.18) | collective-permute-done | bytes 196640 | tf_op jit(solution)/shard_map/ppermute | solution.py:277
  181.7 12.6 %collective-permute-done.20 = bf16[384,256]{1,0:T(8,128)(2,1)} collective-permute-done((bf16[384,256]{1,0:T(8,128)(2,1)}, bf16[384,256]{1,0:T(8,128)(2,1)}, u32[]{:S(2)}, u32[]{:S(2)}) %collective-permute-start.20) | collective-permute-done | bytes 196640 | tf_op jit(solution)/shard_map/ppermute | solution.py:277
  196.2 4.7 %copy-done.7 = bf16[6,2048,512]{2,1,0:T(8,128)(2,1)S(1)} copy-done((bf16[6,2048,512]{2,1,0:T(8,128)(2,1)S(1)}, bf16[6,2048,512]{2,1,0:T(8,128)(2,1)}, u32[]{:S(2)}) %copy-start.7) | copy-done | bytes 12582936
  205.4 8.4 %shard_map.127.q0 = s16[1552,256]{1,0:T(8,128)(2,1)S(1)} custom-call(s32[3,96]{1,0:T(4,128)S(1)} %pad_add_fusion.tab, s32[1]{0:T(128)} %bitcast.6.base, bf16[8,32,512]{2,1,0:T(8,128)(2,1)S(1)} %bitcast.50, bf16[6,2048,512]{2,1,0:T(8,128)(2,1)S(1)} %copy-done.7, bf16[6,2048,512]{2,1,0:T(8,128)(2,1)S(1)} %copy-done.15), custom_call_target="tpu_custom_call" | custom-call | flops 402653184 | bytes 3932160 | tf_op jit(solution)/shard_map/pallas_call | solution.py:70
  240.2 8.6 %collective-permute-done.8 = bf16[384,256]{1,0:T(8,128)(2,1)S(1)} collective-permute-done((bf16[384,256]{1,0:T(8,128)(2,1)S(1)}, bf16[384,256]{1,0:T(8,128)(2,1)S(1)}, u32[]{:S(2)}, u32[]{:S(2)}) %collective-permute-start.8) | collective-permute-done | bytes 196640 | tf_op jit(solution)/shard_map/ppermute | solution.py:277
  253.8 14.6 %collective-permute-done.23.refs_7_ = bf16[1536,256]{1,0:T(8,128)(2,1)} collective-permute-done((bf16[1536,256]{1,0:T(8,128)(2,1)S(1)}, bf16[1536,256]{1,0:T(8,128)(2,1)}, u32[]{:S(2)}, u32[]{:S(2)}) %collective-permute-start.23) | collective-permute-done | bytes 786464 | tf_op jit(solution)/shard_map/ppermute | solution.py:277
  270.9 30.4 %shard_map.139 = f32[6,128,64]{2,1,0:T(8,128)S(1)} custom-call(s32[3,96]{1,0:T(4,128)S(1)} %pad_add_fusion.tab, s32[7]{0:T(128)S(1)} %pad_add_fusion.1.heads, s32[32]{0:T(128)S(1)} %concatenate.19.place, bf16[1536,256]{1,0:T(8,128)(2,1)S(1)} %pad_maximum_fusion.refs_0_, bf16[1536,256]{1,0:T(8,128)(2,1)} %collective-permute-done.9.refs_1_, ...), custom_call_target="tpu_custom_call" | custom-call | flops 3221225472 | bytes 31457280 | tf_op jit(solution)/shard_map/pallas_call | solution.py:228
  301.5 14.5 %all_to_all.5 = f32[16,1,3072]{2,1,0:T(1,128)S(1)} all-to-all(f32[16,1,3072]{2,1,0:T(1,128)S(1)} %reshape.128), channel_id=1, replica_groups=mesh['x'=4,'core'=2,'z'=4,'y'=4] {'z','y'}, dimensions={0} | all-to-all | bytes 393216 | tf_op jit(solution)/shard_map/all_to_all | solution.py:314
  317.9 8.6 %psum.14 = f32[6]{0:T(128)S(1)} all-reduce(f32[6]{0:T(128)S(1)} %multiply_reduce_fusion), channel_id=1, replica_groups=mesh['x'=4,'core'=2,'z'=4,'y'=4] {'y'}, use_global_device_ids=true, to_apply=%region_6.7 | all-reduce | flops 6 | bytes 48 | tf_op jit(solution)/shard_map/psum | solution.py:315
  326.6 8.8 %psum.15 = f32[6]{0:T(128)S(1)} all-reduce(f32[6]{0:T(128)S(1)} %psum.14), channel_id=1, replica_groups=mesh['x'=4,'core'=2,'z'=4,'y'=4] {'z'}, use_global_device_ids=true, to_apply=%region_7.8 | all-reduce | flops 6 | bytes 48 | tf_op jit(solution)/shard_map/psum | solution.py:315
  (137 shorter events, 107.9 us)
Async XLA Ops:
  6.5 247.2 %all-gather.4.cloned.1.call-start = ((), (), s32[]{:S(2)}) async-start(), calls=%async_computation.1 | async-start | bytes 1179648 | tf_op jit(solution)/shard_map/all_gather | solution.py:310
  39.4 61.1 %collective-permute-start.12 = (s16[1552,256]{1,0:T(8,128)(2,1)S(1)}, s16[1552,256]{1,0:T(8,128)(2,1)S(1)}, u32[]{:S(2)}, u32[]{:S(2)}) collective-permute-start(s16[1552,256]{1,0:T(8,128)(2,1)S(1)} %shard_map.134), channel_id=1, source_target_pairs={{0,4},{4,8},{8,12},{12,0},{1,5},{5,9},{9,13},{13,1},{2,6},{6,10},{... | collective-permute-start | bytes 2383880 | tf_op jit(solution)/shard_map/ppermute | solution.py:277
  59.8 40.7 %collective-permute-start.13 = (s16[1552,256]{1,0:T(8,128)(2,1)}, s16[1552,256]{1,0:T(8,128)(2,1)S(1)}, u32[]{:S(2)}, u32[]{:S(2)}) collective-permute-start(s16[1552,256]{1,0:T(8,128)(2,1)} %shard_map.135), channel_id=1, source_target_pairs={{0,8},{4,12},{8,0},{12,4},{1,9},{5,13},{9,1},{13,5},{2,10},{6,14},... | collective-permute-start | bytes 2383880 | tf_op jit(solution)/shard_map/ppermute | solution.py:277
  81.8 19.7 %collective-permute-start.14 = (s16[1552,256]{1,0:T(8,128)(2,1)}, s16[1552,256]{1,0:T(8,128)(2,1)S(1)}, u32[]{:S(2)}, u32[]{:S(2)}) collective-permute-start(s16[1552,256]{1,0:T(8,128)(2,1)} %shard_map.136), channel_id=1, source_target_pairs={{0,12},{4,0},{8,4},{12,8},{1,13},{5,1},{9,5},{13,9},{2,14},{6,2},{... | collective-permute-start | bytes 2383880 | tf_op jit(solution)/shard_map/ppermute | solution.py:277
  104.7 62.7 %collective-permute-start.15 = (s16[400,256]{1,0:T(8,128)(2,1)}, s16[400,256]{1,0:T(8,128)(2,1)S(1)}, u32[]{:S(2)}, u32[]{:S(2)}) collective-permute-start(s16[400,256]{1,0:T(8,128)(2,1)} %get-tuple-element.18), channel_id=1, source_target_pairs={{0,1},{1,2},{2,3},{3,0},{4,5},{5,6},{6,7},{7,4},{8,9},{9,10},{10,1... | collective-permute-start | bytes 614408 | tf_op jit(solution)/shard_map/ppermute | solution.py:277
  106.3 63.1 %collective-permute-start.16 = (s16[400,256]{1,0:T(8,128)(2,1)}, s16[400,256]{1,0:T(8,128)(2,1)S(1)}, u32[]{:S(2)}, u32[]{:S(2)}) collective-permute-start(s16[400,256]{1,0:T(8,128)(2,1)} %get-tuple-element.19), channel_id=1, source_target_pairs={{0,2},{1,3},{2,0},{3,1},{4,6},{5,7},{6,4},{7,5},{8,10},{9,11},{10,... | collective-permute-start | bytes 614408 | tf_op jit(solution)/shard_map/ppermute | solution.py:277
  109.2 60.2 %collective-permute-start.17 = (s16[400,256]{1,0:T(8,128)(2,1)}, s16[400,256]{1,0:T(8,128)(2,1)S(1)}, u32[]{:S(2)}, u32[]{:S(2)}) collective-permute-start(s16[400,256]{1,0:T(8,128)(2,1)} %get-tuple-element.20), channel_id=1, source_target_pairs={{0,3},{1,0},{2,1},{3,2},{4,7},{5,4},{6,5},{7,6},{8,11},{9,8},{10,9... | collective-permute-start | bytes 614408 | tf_op jit(solution)/shard_map/ppermute | solution.py:277
  129.0 84.8 %collective-permute-start = (s16[1552,256]{1,0:T(8,128)(2,1)}, s16[1552,256]{1,0:T(8,128)(2,1)S(1)}, u32[]{:S(2)}, u32[]{:S(2)}) collective-permute-start(s16[1552,256]{1,0:T(8,128)(2,1)} %shard_map.128), channel_id=1, source_target_pairs={{0,1},{1,2},{2,3},{3,0},{4,5},{5,6},{6,7},{7,4},{8,9},{9,10},{10,1... | collective-permute-start | bytes 2383880 | tf_op jit(solution)/shard_map/ppermute | solution.py:277
  148.1 65.7 %collective-permute-start.1 = (s16[1552,256]{1,0:T(8,128)(2,1)}, s16[1552,256]{1,0:T(8,128)(2,1)S(1)}, u32[]{:S(2)}, u32[]{:S(2)}) collective-permute-start(s16[1552,256]{1,0:T(8,128)(2,1)} %shard_map.129), channel_id=1, source_target_pairs={{0,2},{1,3},{2,0},{3,1},{4,6},{5,7},{6,4},{7,5},{8,10},{9,11},{10,... | collective-permute-start | bytes 2383880 | tf_op jit(solution)/shard_map/ppermute | solution.py:277
  167.4 46.4 %collective-permute-start.2 = (s16[1552,256]{1,0:T(8,128)(2,1)}, s16[1552,256]{1,0:T(8,128)(2,1)S(1)}, u32[]{:S(2)}, u32[]{:S(2)}) collective-permute-start(s16[1552,256]{1,0:T(8,128)(2,1)} %shard_map.130), channel_id=1, source_target_pairs={{0,3},{1,0},{2,1},{3,2},{4,7},{5,4},{6,5},{7,6},{8,11},{9,8},{10,9... | collective-permute-start | bytes 2383880 | tf_op jit(solution)/shard_map/ppermute | solution.py:277
  170.3 10.0 %collective-permute-start.18 = (bf16[384,256]{1,0:T(8,128)(2,1)}, bf16[384,256]{1,0:T(8,128)(2,1)S(1)}, u32[]{:S(2)}, u32[]{:S(2)}) collective-permute-start(bf16[384,256]{1,0:T(8,128)(2,1)} %shard_map.138), channel_id=1, source_target_pairs={{0,1},{1,2},{2,3},{3,0},{4,5},{5,6},{6,7},{7,4},{8,9},{9,10},{10,1... | collective-permute-start | bytes 589832 | tf_op jit(solution)/shard_map/ppermute | solution.py:277
  171.0 10.0 %collective-permute-start.19 = (bf16[384,256]{1,0:T(8,128)(2,1)}, bf16[384,256]{1,0:T(8,128)(2,1)S(1)}, u32[]{:S(2)}, u32[]{:S(2)}) collective-permute-start(bf16[384,256]{1,0:T(8,128)(2,1)} %shard_map.138), channel_id=1, source_target_pairs={{0,2},{1,3},{2,0},{3,1},{4,6},{5,7},{6,4},{7,5},{8,10},{9,11},{10,... | collective-permute-start | bytes 589832 | tf_op jit(solution)/shard_map/ppermute | solution.py:277
  180.2 14.0 %collective-permute-start.20 = (bf16[384,256]{1,0:T(8,128)(2,1)}, bf16[384,256]{1,0:T(8,128)(2,1)}, u32[]{:S(2)}, u32[]{:S(2)}) collective-permute-start(bf16[384,256]{1,0:T(8,128)(2,1)} %shard_map.138), channel_id=1, source_target_pairs={{0,3},{1,0},{2,1},{3,2},{4,7},{5,4},{6,5},{7,6},{8,11},{9,8},{10,9... | collective-permute-start | bytes 589832 | tf_op jit(solution)/shard_map/ppermute | solution.py:277
  195.6 54.8 %collective-permute-start.21 = (bf16[1536,256]{1,0:T(8,128)(2,1)S(1)}, bf16[1536,256]{1,0:T(8,128)(2,1)S(1)}, u32[]{:S(2)}, u32[]{:S(2)}) collective-permute-start(bf16[1536,256]{1,0:T(8,128)(2,1)S(1)} %pad_maximum_fusion.1.refs_4_), channel_id=1, source_target_pairs={{0,4},{4,8},{8,12},{12,0},{1,5},{5,9},{9,13},{13,1},{2,6},{6,10},{... | collective-permute-start | bytes 2359304 | tf_op jit(solution)/shard_map/ppermute | solution.py:277
  215.6 7.7 %collective-permute-start.3 = (s16[400,256]{1,0:T(8,128)(2,1)S(1)}, s16[400,256]{1,0:T(8,128)(2,1)S(1)}, u32[]{:S(2)}, u32[]{:S(2)}) collective-permute-start(s16[400,256]{1,0:T(8,128)(2,1)S(1)} %get-tuple-element.14), channel_id=1, source_target_pairs={{0,4},{4,8},{8,12},{12,0},{1,5},{5,9},{9,13},{13,1},{2,6},{6,10},{... | collective-permute-start | bytes 614408 | tf_op jit(solution)/shard_map/ppermute | solution.py:277
  216.1 9.7 %collective-permute-start.4 = (s16[400,256]{1,0:T(8,128)(2,1)S(1)}, s16[400,256]{1,0:T(8,128)(2,1)S(1)}, u32[]{:S(2)}, u32[]{:S(2)}) collective-permute-start(s16[400,256]{1,0:T(8,128)(2,1)S(1)} %get-tuple-element.15), channel_id=1, source_target_pairs={{0,8},{4,12},{8,0},{12,4},{1,9},{5,13},{9,1},{13,5},{2,10},{6,14},... | collective-permute-start | bytes 614408 | tf_op jit(solution)/shard_map/ppermute | solution.py:277
  226.0 10.0 %collective-permute-start.6 = (bf16[384,256]{1,0:T(8,128)(2,1)S(1)}, bf16[384,256]{1,0:T(8,128)(2,1)S(1)}, u32[]{:S(2)}, u32[]{:S(2)}) collective-permute-start(bf16[384,256]{1,0:T(8,128)(2,1)S(1)} %shard_map.132), channel_id=1, source_target_pairs={{0,4},{4,8},{8,12},{12,0},{1,5},{5,9},{9,13},{13,1},{2,6},{6,10},{... | collective-permute-start | bytes 589832 | tf_op jit(solution)/shard_map/ppermute | solution.py:277
  228.0 12.2 %collective-permute-start.7 = (bf16[384,256]{1,0:T(8,128)(2,1)S(1)}, bf16[384,256]{1,0:T(8,128)(2,1)S(1)}, u32[]{:S(2)}, u32[]{:S(2)}) collective-permute-start(bf16[384,256]{1,0:T(8,128)(2,1)S(1)} %shard_map.132), channel_id=1, source_target_pairs={{0,8},{4,12},{8,0},{12,4},{1,9},{5,13},{9,1},{13,5},{2,10},{6,14},... | collective-permute-start | bytes 589832 | tf_op jit(solution)/shard_map/ppermute | solution.py:277
  230.2 18.6 %collective-permute-start.8 = (bf16[384,256]{1,0:T(8,128)(2,1)S(1)}, bf16[384,256]{1,0:T(8,128)(2,1)S(1)}, u32[]{:S(2)}, u32[]{:S(2)}) collective-permute-start(bf16[384,256]{1,0:T(8,128)(2,1)S(1)} %shard_map.132), channel_id=1, source_target_pairs={{0,12},{4,0},{8,4},{12,8},{1,13},{5,1},{9,5},{13,9},{2,14},{6,2},{... | collective-permute-start | bytes 589832 | tf_op jit(solution)/shard_map/ppermute | solution.py:277
  231.8 21.9 %collective-permute-start.22 = (bf16[1536,256]{1,0:T(8,128)(2,1)S(1)}, bf16[1536,256]{1,0:T(8,128)(2,1)}, u32[]{:S(2)}, u32[]{:S(2)}) collective-permute-start(bf16[1536,256]{1,0:T(8,128)(2,1)S(1)} %pad_maximum_fusion.1.refs_4_), channel_id=1, source_target_pairs={{0,8},{4,12},{8,0},{12,4},{1,9},{5,13},{9,1},{13,5},{2,10},{6,14},... | collective-permute-start | bytes 2359304 | tf_op jit(solution)/shard_map/ppermute | solution.py:277
  236.0 32.4 %collective-permute-start.23 = (bf16[1536,256]{1,0:T(8,128)(2,1)S(1)}, bf16[1536,256]{1,0:T(8,128)(2,1)}, u32[]{:S(2)}, u32[]{:S(2)}) collective-permute-start(bf16[1536,256]{1,0:T(8,128)(2,1)S(1)} %pad_maximum_fusion.1.refs_4_), channel_id=1, source_target_pairs={{0,12},{4,0},{8,4},{12,8},{1,13},{5,1},{9,5},{13,9},{2,14},{6,2},{... | collective-permute-start | bytes 2359304 | tf_op jit(solution)/shard_map/ppermute | solution.py:277
  248.8 19.6 %collective-permute-start.10 = (bf16[1536,256]{1,0:T(8,128)(2,1)S(1)}, bf16[1536,256]{1,0:T(8,128)(2,1)}, u32[]{:S(2)}, u32[]{:S(2)}) collective-permute-start(bf16[1536,256]{1,0:T(8,128)(2,1)S(1)} %pad_maximum_fusion.refs_0_), channel_id=1, source_target_pairs={{0,2},{1,3},{2,0},{3,1},{4,6},{5,7},{6,4},{7,5},{8,10},{9,11},{10,... | collective-permute-start | bytes 2359304 | tf_op jit(solution)/shard_map/ppermute | solution.py:277
  250.2 18.2 %collective-permute-start.11 = (bf16[1536,256]{1,0:T(8,128)(2,1)S(1)}, bf16[1536,256]{1,0:T(8,128)(2,1)}, u32[]{:S(2)}, u32[]{:S(2)}) collective-permute-start(bf16[1536,256]{1,0:T(8,128)(2,1)S(1)} %pad_maximum_fusion.refs_0_), channel_id=1, source_target_pairs={{0,3},{1,0},{2,1},{3,2},{4,7},{5,4},{6,5},{7,6},{8,11},{9,8},{10,9... | collective-permute-start | bytes 2359304 | tf_op jit(solution)/shard_map/ppermute | solution.py:277
  251.3 19.6 %collective-permute-start.9 = (bf16[1536,256]{1,0:T(8,128)(2,1)S(1)}, bf16[1536,256]{1,0:T(8,128)(2,1)}, u32[]{:S(2)}, u32[]{:S(2)}) collective-permute-start(bf16[1536,256]{1,0:T(8,128)(2,1)S(1)} %pad_maximum_fusion.refs_0_), channel_id=1, source_target_pairs={{0,1},{1,2},{2,3},{3,0},{4,5},{5,6},{6,7},{7,4},{8,9},{9,10},{10,1... | collective-permute-start | bytes 2359304 | tf_op jit(solution)/shard_map/ppermute | solution.py:277
  (31 other events, 320.3 us)
Sparse Core Ops, SparseCore 0:
  181.1 20.6 all-gather.3

commit v2 on v0

v2 whole, which is shorter than its diff:
```python
import functools

import jax
import jax.numpy as jnp
from jax import lax
from jax.experimental import pallas as pl
from jax.experimental.pallas import tpu as pltpu
from jax.sharding import Mesh, PartitionSpec as P

BLK = 128
FOOT = 32
RES = 128.0
TOP = 32767.0
MIB = 1024 * 1024
VMEM = pltpu.VMEM
SMEM = pltpu.SMEM
F32 = jnp.float32
BF16 = jnp.bfloat16
I16 = jnp.int16
I32 = jnp.int32


def scale_code(peak):
    return jnp.ceil(jnp.log(jnp.maximum(peak, 1e-30)) * (RES / 0.6931471805599453)) + 1.0


def scale_of(code):
    return jnp.exp2(code * (1.0 / RES))


def encode(x):
    code = scale_code(jnp.max(jnp.abs(x), axis=0, keepdims=True))
    q = jnp.round(x * (TOP / scale_of(code)))
    return q.astype(I32).astype(I16), code


def position():
    y, z = lax.axis_index("y").astype(I32), lax.axis_index("z").astype(I32)
    zero = lax.axis_index("core") == 0
    return jnp.where(zero, y, z), jnp.where(zero, z, y)


def block_counts(lens):
    return [(lens[e] + (BLK - 1)) // BLK for e in range(lens.shape[0])]


def locate(b, lens):
    n = lens.shape[0]
    start, e, end = jnp.int32(0), jnp.int32(0), jnp.int32(0)
    for count in block_counts(lens):
        end = end + count
        past = b >= end
        start = jnp.where(past, end, start)
        e = jnp.where(past, e + 1, e)
    inside = e < n
    e = jnp.minimum(e, n - 1)
    t = jnp.where(inside, (b - start) * BLK, 0)
    return e, t, jnp.where(inside, jnp.clip(lens[e] - t, 0, BLK), 0)


def dp_place():
    return lax.axis_index("x").astype(I32) * 2 + lax.axis_index("core").astype(I32)


def ring_of(x):
    n = 8
    others = [
        lax.ppermute(x, ("x", "core"), [(i, (i + s) % n) for i in range(n)]) for s in range(1, n)
    ]
    return [x] + others


def load_kernel(a_hbm, g_hbm, a, g, sems):
    copies = [
        pltpu.make_async_copy(a_hbm, a, sems.at[0]),
        pltpu.make_async_copy(g_hbm, g, sems.at[1]),
    ]
    for c in copies:
        c.start()
    for c in copies:
        c.wait()


def load(a, g):
    return pl.pallas_call(
        load_kernel,
        out_shape=[VMEM(a.shape, a.dtype), VMEM(g.shape, g.dtype)],
        in_specs=[pl.BlockSpec(memory_space=pl.ANY)] * 2,
        out_specs=[pl.BlockSpec(memory_space=VMEM)] * 2,
        scratch_shapes=[pltpu.SemaphoreType.DMA((2,))],
        compiler_params=pltpu.CompilerParams(vmem_limit_bytes=24 * MIB),
        cost_estimate=pl.CostEstimate(flops=0, bytes_accessed=a.size * 4, transcendentals=0),
    )(a, g)


def turn_kernel(*refs):
    parts, (w, flat) = refs[:8], refs[8:]
    me = dp_place()
    rank = parts[0].shape[1]
    for s, part in enumerate(parts):
        at = pl.ds(pl.multiple_of((me - s) % 8 * rank, rank), rank)
        for i in range(2):
            flat[i, at, :] = part[i]
    for i in range(2):
        w[i] = flat[i].T


def turn(parts):
    _, rank, width = parts[0].shape
    return pl.pallas_call(
        turn_kernel,
        out_shape=jax.ShapeDtypeStruct((2, width, 8 * rank), BF16),
        in_specs=[pl.BlockSpec(memory_space=VMEM)] * 8,
        out_specs=pl.BlockSpec(memory_space=VMEM),
        scratch_shapes=[VMEM((2, 8 * rank, width), BF16)],
        compiler_params=pltpu.CompilerParams(vmem_limit_bytes=4 * MIB),
    )(*parts)


def foot(ref, start, codes, count):
    rows = [codes[k] for k in range(count)]
    rows.append(jnp.zeros((FOOT - count, 256), F32))
    ref[start:, :] = jnp.concatenate(rows, axis=0).astype(I32).astype(I16)


def partial_kernel(nblk, s, lens, w, a, g, q, codes):
    first = (position()[0] + s) % 4 * nblk

    def block(k, carry):
        e, t, count = locate(first + k, lens)
        t = pl.multiple_of(t, BLK)
        at = pl.ds(pl.multiple_of(k * BLK, BLK), BLK)
        live = lax.broadcasted_iota(I32, (BLK, 128), 0) < count
        for i, rows in enumerate((a, g)):
            x = jnp.dot(rows[e, pl.ds(t, BLK), :], w[i], preferred_element_type=F32)
            x = jnp.where(live, x, 0.0)
            coded, code = encode(x)
            q[at, i * 128 : (i + 1) * 128] = coded
            codes[k, :, i * 128 : (i + 1) * 128] = code
        return carry

    lax.fori_loop(0, nblk, block, 0, unroll=4)
    foot(q, nblk * BLK, codes, nblk)


def partial_piece(lens, w, a, g, nblk, s):
    rows = nblk * BLK
    return pl.pallas_call(
        functools.partial(partial_kernel, nblk, s),
        out_shape=jax.ShapeDtypeStruct((rows + FOOT, 256), I16),
        in_specs=[pl.BlockSpec(memory_space=SMEM)] + [pl.BlockSpec(memory_space=VMEM)] * 3,
        out_specs=pl.BlockSpec(memory_space=VMEM),
        scratch_shapes=[VMEM((FOOT, 1, 256), F32)],
        compiler_params=pltpu.CompilerParams(vmem_limit_bytes=6 * MIB),
        cost_estimate=pl.CostEstimate(
            flops=16 * rows * 512 * 128, bytes_accessed=rows * 2048, transcendentals=0
        ),
    )(lens, w, a, g)


def scales_of(refs, rows, count):
    return [scale_of(r[rows:, :].astype(I32).astype(F32)) * (1.0 / TOP) for r in refs]


def value(ref, start, n):
    return ref[pl.ds(start, n), :].astype(I32).astype(F32)


def middle_kernel(rows, sub, step, which, q0, q1, q2, q3, *rest):
    refs, outs, (scales, codes) = (q0, q1, q2, q3), rest[:-2], rest[-2:]
    two = position()[1]
    for i, s in enumerate(scales_of(refs, rows, rows // BLK)):
        scales[i] = s
    for s, out in zip(which, outs):
        begin = (two + s) % 4 * sub

        def some(j, carry, out=out, begin=begin):
            at = pl.multiple_of(begin + j * step, step)
            total = None
            for i, r in enumerate(refs):
                v = value(r, at, step) * scales[i, pl.ds(at // BLK, 1), :]
                total = v if total is None else total + v
            coded, code = encode(total)
            out[pl.ds(pl.multiple_of(j * step, step), step), :] = coded
            codes[j] = code
            return carry

        lax.fori_loop(0, sub // step, some, 0, unroll=4)
        foot(out, sub, codes, sub // step)


def middle_sum(pieces, rows, sub, step, which):
    return pl.pallas_call(
        functools.partial(middle_kernel, rows, sub, step, which),
        out_shape=[jax.ShapeDtypeStruct((sub + FOOT, 256), I16)] * len(which),
        in_specs=[pl.BlockSpec(memory_space=VMEM)] * 4,
        out_specs=[pl.BlockSpec(memory_space=VMEM)] * len(which),
        scratch_shapes=[VMEM((4, FOOT, 256), F32), VMEM((FOOT, 1, 256), F32)],
        compiler_params=pltpu.CompilerParams(vmem_limit_bytes=10 * MIB),
        cost_estimate=pl.CostEstimate(
            flops=rows * 64 * 8 * len(which), bytes_accessed=rows * 256 * 2, transcendentals=0
        ),
    )(*pieces)


def last_kernel(sub, step, r0, r1, r2, r3, out):
    refs = (r0, r1, r2, r3)
    scales = scales_of(refs, sub, sub // step)
    for j in range(sub // step):
        total = None
        for i, r in enumerate(refs):
            v = value(r, j * step, step) * scales[i][j : j + 1, :]
            total = v if total is None else total + v
        out[j * step : (j + 1) * step, :] = total.astype(BF16)


def last_sum(pieces, sub, step):
    return pl.pallas_call(
        functools.partial(last_kernel, sub, step),
        out_shape=jax.ShapeDtypeStruct((sub, 256), BF16),
        in_specs=[pl.BlockSpec(memory_space=VMEM)] * 4,
        out_specs=pl.BlockSpec(memory_space=VMEM),
        compiler_params=pltpu.CompilerParams(vmem_limit_bytes=6 * MIB),
        cost_estimate=pl.CostEstimate(
            flops=sub * 256 * 8, bytes_accessed=sub * 256 * 10, transcendentals=0
        ),
    )(*pieces)


def precondition(grad, first, second):
    top = 0.9 * first + 0.1 * grad
    return top / (jnp.sqrt(0.999 * second + 0.001 * grad * grad) + 1e-08)


def join_kernel(r0, r1, r2, r3, out):
    two = position()[1]
    for s, r in enumerate((r0, r1, r2, r3)):
        out[(two - s) % 4] = r[...]


def join(parts):
    sub = parts[0].shape[0]
    return pl.pallas_call(
        join_kernel,
        out_shape=jax.ShapeDtypeStruct((4, sub, 256), BF16),
        in_specs=[pl.BlockSpec(memory_space=VMEM)] * 4,
        out_specs=pl.BlockSpec(memory_space=VMEM),
        compiler_params=pltpu.CompilerParams(vmem_limit_bytes=8 * MIB),
    )(*parts).reshape(4 * sub, 256)


def gather_sums(which, nblk, lens, pieces, a, g, up, down):
    tn = (((0,), (0,)), ((), ()))
    one = position()[0]
    for s, piece in zip(which, pieces):
        low = (one - s) % 4 * nblk

        def example(e, begin, piece=piece, low=low):
            count = (lens[e] + (BLK - 1)) // BLK
            first = jnp.clip(begin - low, 0, nblk)
            some = jnp.clip(begin + count - low, 0, nblk) - first
            skip = jnp.maximum(low - begin, 0)

            def add(b, n):
                packed = pl.ds(pl.multiple_of((first + b) * BLK, BLK), n * BLK)
                rows = pl.ds(pl.multiple_of((skip + b) * BLK, BLK), n * BLK)
                up[e] += lax.dot_general(
                    piece[packed, :128], g[e, rows, :], tn, preferred_element_type=F32
                )
                down[e] += lax.dot_general(
                    piece[packed, 128:], a[e, rows, :], tn, preferred_element_type=F32
                )

            for n in (16, 8, 4, 2, 1):

                @pl.when((some // n) % 2 == 1)
                def _(n=n):
                    add(some // (2 * n) * (2 * n), n)

            return begin + count

        lax.fori_loop(0, 6, example, jnp.int32(0))


def early_kernel(which, nblk, lens, *refs):
    n = len(which)
    a, g, up, down = refs[n:]
    up[...] = jnp.zeros_like(up)
    down[...] = jnp.zeros_like(down)
    gather_sums(which, nblk, lens, refs[:n], a, g, up, down)


def early_grads(which, nblk, lens, pieces, a, g):
    grad = jax.ShapeDtypeStruct((6, 128, 512), F32)
    return pl.pallas_call(
        functools.partial(early_kernel, which, nblk),
        out_shape=[grad, grad],
        in_specs=[pl.BlockSpec(memory_space=SMEM)]
        + [pl.BlockSpec(memory_space=VMEM)] * (len(which) + 2),
        out_specs=[pl.BlockSpec(memory_space=VMEM)] * 2,
        compiler_params=pltpu.CompilerParams(vmem_limit_bytes=6 * MIB),
        cost_estimate=pl.CostEstimate(
            flops=4 * nblk * len(which) * BLK * 512 * 128,
            bytes_accessed=nblk * len(which) * BLK * 512,
            transcendentals=0,
        ),
    )(lens, *pieces, a, g)


def final_kernel(which, nblk, lens, *refs):
    n = len(which)
    a, g, up0, down0 = refs[n : n + 4]
    parts = refs[n + 4 : n + 12]
    urp, uwp, dwp, drp, out, up, down, moments = refs[n + 12 :]
    nt = (((1,), (1,)), ((), ()))
    high = lax.Precision.HIGHEST
    me = dp_place()
    rank = parts[0].shape[0] // 4
    for s, part in enumerate(parts):
        at = pl.ds(pl.multiple_of((me - s) % 8 * rank, rank), rank)
        for i in range(4):
            moments[i, at, :] = part[i * rank : (i + 1) * rank, :]
    up[...] = up0[...]
    down[...] = down0[...]
    gather_sums(which, nblk, lens, refs[:n], a, g, up, down)

    def example(e, carry):
        for i, (grad, width, side) in enumerate(((up, uwp, urp), (down, dwp, drp))):
            pre = precondition(grad[e], moments[2 * i], moments[2 * i + 1])
            wide = lax.dot_general(
                pre, width[...], nt, precision=high, preferred_element_type=F32
            )
            out[e, i * 64 : (i + 1) * 64, :] = jnp.dot(
                side[...], wide, precision=high, preferred_element_type=F32
            )
        return carry

    lax.fori_loop(0, 6, example, 0)


def final_grads(which, nblk, lens, pieces, a, g, up, down, moments, *projectors):
    return pl.pallas_call(
        functools.partial(final_kernel, which, nblk),
        out_shape=jax.ShapeDtypeStruct((6, 128, 64), F32),
        in_specs=[pl.BlockSpec(memory_space=SMEM)]
        + [pl.BlockSpec(memory_space=VMEM)] * (len(which) + 16),
        out_specs=pl.BlockSpec(memory_space=VMEM),
        scratch_shapes=[
            VMEM((6, 128, 512), F32),
            VMEM((6, 128, 512), F32),
            VMEM((4, 128, 512), F32),
        ],
        compiler_params=pltpu.CompilerParams(vmem_limit_bytes=10 * MIB),
        cost_estimate=pl.CostEstimate(
            flops=4 * nblk * len(which) * BLK * 512 * 128,
            bytes_accessed=nblk * len(which) * BLK * 512,
            transcendentals=0,
        ),
    )(lens, *pieces, a, g, up, down, *moments, *projectors)


def shifts(first, s):
    pairs = []
    for core in range(2):
        for z in range(4):
            for y in range(4):
                along_y = (core == 0) == first
                to = (z, (y + s) % 4) if along_y else ((z + s) % 4, y)
                pairs.append((core * 16 + z * 4 + y, core * 16 + to[0] * 4 + to[1]))
    return pairs


def send(x, first, s):
    return x if s == 0 else lax.ppermute(x, ("core", "z", "y"), shifts(first, s))


def features(nb, lens, w, moments, a, g, projectors):
    rows, sub, step, per = nb * BLK // 4, nb * BLK // 16, 32, nb // 4
    got = [None] * 4
    for s in (2, 1, 3, 0):
        got[s] = send(partial_piece(lens, w, a, g, per, s), True, s)
    got[0], moments = lax.optimization_barrier((got[0], moments))
    ring = ring_of(moments)
    back = [None] * 4
    for which in ((2,), (1, 3, 0)):
        for s, mid in zip(which, middle_sum(got, rows, sub, step, which)):
            back[s] = send(mid, False, s)
    own = last_sum(back, sub, step)
    piece = join([send(own, False, s) for s in range(4)])
    pieces = {s: send(piece, True, s) for s in (0, 1, 3, 2)}
    soon, late = (0, 1, 3), (2,)
    up, down = early_grads(soon, per, lens, [pieces[s] for s in soon], a, g)
    return final_grads(
        late, per, lens, [pieces[s] for s in late], a, g, up, down, ring, *projectors
    )


def share(x, axes, n):
    return lax.all_to_all(jnp.broadcast_to(x[None], (n,) + x.shape), axes, 0, 0, tiled=True)


def body(a, g, lengths, sf, ef, sra, srv, era, erv, urp, uwp, dwp, drp):
    param = ("z", "y")
    w = turn(ring_of(jnp.stack([sf.T, ef])))
    a, g = load(a, g)
    moments = jnp.concatenate([era, erv, sra.T, srv.T], axis=0)
    nb = a.shape[0] * a.shape[1] // BLK
    part = features(nb, lengths, w, moments, a, g, (urp.T, uwp.T, dwp.T, drp.T))
    owned = jnp.swapaxes(part.reshape(6, 16, 8, 64), 0, 1)
    raw = jnp.sum(lax.all_to_all(owned, param, 0, 0, tiled=True), axis=0)
    square = jnp.sum(raw * raw, axis=(1, 2))
    square = share(jnp.broadcast_to(square[:, None], (6, 128)), param, 16)
    scale = lax.rsqrt(jnp.sum(square, axis=0)[:, 0] / 8192.0 + 1e-06)
    return (raw * scale[:, None, None]).reshape(6, 512)


def solution(mesh):
    grid = Mesh(mesh.devices.reshape(4, 2, 4, 4), ("x", "core", "z", "y"))
    dp, param = ("x", "core"), ("z", "y")
    in_specs = (
        P(dp, None, param),
        P(dp, None, param),
        P(dp),
        P(param, dp),
        P(dp, param),
        P(param, dp),
        P(param, dp),
        P(dp, param),
        P(dp, param),
        P(),
        P(param, None),
        P(param, None),
        P(),
    )
    return jax.shard_map(body, mesh=grid, in_specs=in_specs, out_specs=P(dp, param), check_vma=False)
```

time: 496 us -> 188 us (0.38)
  blocking collectives: 356 us -> 13.7 us
  Pallas kernels: 0 us -> 43.3 us
  matrix products: 38 us -> 0 us
  starting transfers between devices: 0.01 us -> 37.2 us
  between operations: 13.6 us -> 0.37 us
    psum x1 -> x0, blocking collectives: 278 us -> none  [body(): low_sum, rise_sum = lax.psum((low_part, rise_part), 'param')]
    psum x1 -> x0, waiting for transfers between devices: 84 us -> none  [body(): summed = lax.psum(partial_value, 'param')]
    ppermute x0 -> x26, waiting for transfers between devices: none -> 80.2 us  [the longest x12 72.3 us: send(): lax.ppermute(x, ('core', 'z', 'y'), shifts(first, s))]
    all_gather x6 -> x0, blocking collectives: 77.3 us -> none  [the longest x1 13.1 us: body(): lax.all_gather(expanding_factor, 'dp', axis=0, tiled=True)]
    pallas_call x0 -> x12, Pallas kernels: none -> 43.3 us  [the longest x4 14.4 us: partial_piece(): pl.pallas_call(functools.partial(partial_kernel, nblk, s), out_shape=jax....]
    dot_general x8 -> x0, matrix products: 38 us -> none  [the longest x1 11.5 us: body(): jnp.einsum('etd,rd->etr', output_gradient_rows, up_cols, preferred_elemen...]
    ppermute x0 -> x26, starting transfers between devices: none -> 33.7 us  [the longest x12 20.2 us: send(): lax.ppermute(x, ('core', 'z', 'y'), shifts(first, s))]
    all_to_all x0 -> x1, blocking collectives: none -> 13.7 us  [body(): raw = jnp.sum(lax.all_to_all(owned, param, 0, 0, tiled=True), axis=0)]
  transfers between devices with their start and end apart: 1 -> 27, of which waited for: 1 -> 11; matrix products, arithmetic and copies ran while one was open for 0% -> 0% of each run, Pallas kernels for 0% -> 11%
where the time goes in v2:
time: 188 us; the launch traced here: 187 us
  waiting for transfers between devices  87.7 us (47%)
  Pallas kernels  43.3 us (23%)
  starting transfers between devices  37.2 us (20%)
  blocking collectives  13.7 us (7%)
  other arithmetic  2.85 us (2%)
    ppermute x12, waiting for transfers between devices, send(): lax.ppermute(x, ('core', 'z', 'y'), shifts(first, s))  72.3 us
    ppermute x12, starting transfers between devices, send(): lax.ppermute(x, ('core', 'z', 'y'), shifts(first, s))  20.2 us
    pallas_call x4, Pallas kernels, partial_piece(): pl.pallas_call(functools.partial(partial_kernel, nblk, s), out_shape=jax....  14.4 us
    all_to_all x1, blocking collectives, body(): raw = jnp.sum(lax.all_to_all(owned, param, 0, 0, tiled=True), axis=0)  13.7 us
    ppermute x14, starting transfers between devices, ring_of(): lax.ppermute(x, ('x', 'core'), [(i, (i + s) % n) for i in range(n)])  13.5 us
    pallas_call x1, Pallas kernels, final_grads(): pl.pallas_call(functools.partial(final_kernel, which, nblk), out_shape=ja...  11 us
    pallas_call x1, Pallas kernels, load(): pl.pallas_call(load_kernel, out_shape=[VMEM(a.shape, a.dtype), VMEM(g.sha...  8.17 us
    ppermute x14, waiting for transfers between devices, ring_of(): lax.ppermute(x, ('x', 'core'), [(i, (i + s) % n) for i in range(n)])  7.89 us
  transfers between devices with their start and end apart: 27, of which 11 were waited for; matrix products, arithmetic and copies ran while one was open for 0% of the time, Pallas kernels for 11%

profile of v2, /device:TPU:6, one launch (start us, length us, event | category | flops | bytes accessed | tf_op | source)
XLA Modules:
  0.0 186.8 jit_solution(13245044927858095426)
XLA Ops:
  1.2 2.4 %collective-permute-start.2 = (bf16[2,16,512]{2,1,0:T(8,128)(2,1)S(1)}, bf16[2,16,512]{2,1,0:T(8,128)(2,1)S(1)}, u32[]{:S(2)}, u32[]{:S(2)}) collective-permute-start(bf16[2,16,512]{2,1,0:T(8,128)(2,1)S(1)} %pad_maximum_fusion.1.refs_0_), channel_id=1, source_target_pairs={{0,48},{16,64},{32,80},{48,96},{64,112},{80,0},{96,16},{112,32},{1... | collective-permute-start | bytes 98312 | tf_op jit(solution)/shard_map/ppermute | solution.py:68
  7.7 8.2 %shard_map.128 = (bf16[6,2048,512]{2,1,0:T(8,128)(2,1)S(1)}, bf16[6,2048,512]{2,1,0:T(8,128)(2,1)S(1)}) custom-call(bf16[6,2048,512]{2,1,0:T(8,128)(2,1)} %a_hbm.1, bf16[6,2048,512]{2,1,0:T(8,128)(2,1)} %g_hbm.1), custom_call_target="tpu_custom_call" | custom-call | bytes 25165824 | tf_op jit(solution)/shard_map/pallas_call | solution.py:85
  16.1 3.6 %shard_map.132 = s16[3104,256]{1,0:T(8,128)(2,1)S(1)} custom-call(s32[6]{0:T(128)S(1)} %copy-done.6, bf16[2,512,128]{2,1,0:T(8,128)(2,1)S(1)} %shard_map.127.w, bf16[6,2048,512]{2,1,0:T(8,128)(2,1)S(1)} %get-tuple-element.14.a.refs_3_.refs_1_, bf16[6,2048,512]{2,1,0:T(8,128)(2,1)S(1)} %get-tuple-element.15.g.refs_4_.refs_2_), custom_call_target="tpu_custom_call" | custom-call | flops 3221225472 | bytes 6291456 | tf_op jit(solution)/shard_map/pallas_call | solution.py:148
  19.7 3.6 %shard_map.131 = s16[3104,256]{1,0:T(8,128)(2,1)S(1)} custom-call(s32[6]{0:T(128)S(1)} %copy-done.6, bf16[2,512,128]{2,1,0:T(8,128)(2,1)S(1)} %shard_map.127.w, bf16[6,2048,512]{2,1,0:T(8,128)(2,1)S(1)} %get-tuple-element.14.a.refs_3_.refs_1_, bf16[6,2048,512]{2,1,0:T(8,128)(2,1)S(1)} %get-tuple-element.15.g.refs_4_.refs_2_), custom_call_target="tpu_custom_call" | custom-call | flops 3221225472 | bytes 6291456 | tf_op jit(solution)/shard_map/pallas_call | solution.py:148
  23.4 3.6 %shard_map.130 = s16[3104,256]{1,0:T(8,128)(2,1)S(1)} custom-call(s32[6]{0:T(128)S(1)} %copy-done.6, bf16[2,512,128]{2,1,0:T(8,128)(2,1)S(1)} %shard_map.127.w, bf16[6,2048,512]{2,1,0:T(8,128)(2,1)S(1)} %get-tuple-element.14.a.refs_3_.refs_1_, bf16[6,2048,512]{2,1,0:T(8,128)(2,1)S(1)} %get-tuple-element.15.g.refs_4_.refs_2_), custom_call_target="tpu_custom_call" | custom-call | flops 3221225472 | bytes 6291456 | tf_op jit(solution)/shard_map/pallas_call | solution.py:148
  27.0 3.1 %collective-permute-start.9 = (s16[3104,256]{1,0:T(8,128)(2,1)S(1)}, s16[3104,256]{1,0:T(8,128)(2,1)S(1)}, u32[]{:S(2)}, u32[]{:S(2)}) collective-permute-start(s16[3104,256]{1,0:T(8,128)(2,1)S(1)} %shard_map.132), channel_id=1, source_target_pairs={{0,3},{1,0},{2,1},{3,2},{4,7},{5,4},{6,5},{7,6},{8,11},{9,8},{10,9... | collective-permute-start | bytes 4767752 | tf_op jit(solution)/shard_map/ppermute | solution.py:374
  31.7 3.6 %shard_map.129.q0 = s16[3104,256]{1,0:T(8,128)(2,1)S(1)} custom-call(s32[6]{0:T(128)S(1)} %copy-done.6, bf16[2,512,128]{2,1,0:T(8,128)(2,1)S(1)} %shard_map.127.w, bf16[6,2048,512]{2,1,0:T(8,128)(2,1)S(1)} %get-tuple-element.14.a.refs_3_.refs_1_, bf16[6,2048,512]{2,1,0:T(8,128)(2,1)S(1)} %get-tuple-element.15.g.refs_4_.refs_2_), custom_call_target="tpu_custom_call" | custom-call | flops 3221225472 | bytes 6291456 | tf_op jit(solution)/shard_map/pallas_call | solution.py:148
  35.3 29.9 %collective-permute-done.9.q3 = s16[3104,256]{1,0:T(8,128)(2,1)S(1)} collective-permute-done((s16[3104,256]{1,0:T(8,128)(2,1)S(1)}, s16[3104,256]{1,0:T(8,128)(2,1)S(1)}, u32[]{:S(2)}, u32[]{:S(2)}) %collective-permute-start.9) | collective-permute-done | bytes 1589280 | tf_op jit(solution)/shard_map/ppermute | solution.py:374
  65.2 4.0 %collective-permute-done.7.q1 = s16[3104,256]{1,0:T(8,128)(2,1)S(1)} collective-permute-done((s16[3104,256]{1,0:T(8,128)(2,1)S(1)}, s16[3104,256]{1,0:T(8,128)(2,1)S(1)}, u32[]{:S(2)}, u32[]{:S(2)}) %collective-permute-start.7) | collective-permute-done | bytes 1589280 | tf_op jit(solution)/shard_map/ppermute | solution.py:374
  70.0 4.0 %collective-permute-start.11 = (s16[800,256]{1,0:T(8,128)(2,1)S(1)}, s16[800,256]{1,0:T(8,128)(2,1)S(1)}, u32[]{:S(2)}, u32[]{:S(2)}) collective-permute-start(s16[800,256]{1,0:T(8,128)(2,1)S(1)} %shard_map.134), channel_id=1, source_target_pairs={{0,8},{1,9},{2,10},{3,11},{4,12},{5,13},{6,14},{7,15},{8,0},{9,1},... | collective-permute-start | bytes 1228808 | tf_op jit(solution)/shard_map/ppermute | solution.py:374
  74.0 2.4 %shard_map.133 = (s16[800,256]{1,0:T(8,128)(2,1)S(1)}, s16[800,256]{1,0:T(8,128)(2,1)S(1)}, s16[800,256]{1,0:T(8,128)(2,1)S(1)}) custom-call(s16[3104,256]{1,0:T(8,128)(2,1)S(1)} %shard_map.129.q0, s16[3104,256]{1,0:T(8,128)(2,1)S(1)} %collective-permute-done.7.q1, s16[3104,256]{1,0:T(8,128)(2,1)S(1)} %collective-permute-done.8.q2, ...), custom_call_target="tpu_custom_call" | custom-call | flops 4718592 | bytes 1572864 | tf_op jit(solution)/shard_map/pallas_call | solution.py:193
  79.9 5.7 %collective-permute-done.10.r1 = s16[800,256]{1,0:T(8,128)(2,1)S(1)} collective-permute-done((s16[800,256]{1,0:T(8,128)(2,1)S(1)}, s16[800,256]{1,0:T(8,128)(2,1)S(1)}, u32[]{:S(2)}, u32[]{:S(2)}) %collective-permute-start.10) | collective-permute-done | bytes 409632 | tf_op jit(solution)/shard_map/ppermute | solution.py:374
  86.9 3.9 %collective-permute-start.14 = (bf16[768,256]{1,0:T(8,128)(2,1)S(1)}, bf16[768,256]{1,0:T(8,128)(2,1)S(1)}, u32[]{:S(2)}, u32[]{:S(2)}) collective-permute-start(bf16[768,256]{1,0:T(8,128)(2,1)S(1)} %shard_map.135.r0), channel_id=1, source_target_pairs={{0,8},{1,9},{2,10},{3,11},{4,12},{5,13},{6,14},{7,15},{8,0},{9,1},... | collective-permute-start | bytes 1179656 | tf_op jit(solution)/shard_map/ppermute | solution.py:374
  91.0 4.1 %collective-permute-done.13.r1 = bf16[768,256]{1,0:T(8,128)(2,1)S(1)} collective-permute-done((bf16[768,256]{1,0:T(8,128)(2,1)S(1)}, bf16[768,256]{1,0:T(8,128)(2,1)S(1)}, u32[]{:S(2)}, u32[]{:S(2)}) %collective-permute-start.13) | collective-permute-done | bytes 393248 | tf_op jit(solution)/shard_map/ppermute | solution.py:374
  95.1 6.3 %collective-permute-done.14.r2 = bf16[768,256]{1,0:T(8,128)(2,1)S(1)} collective-permute-done((bf16[768,256]{1,0:T(8,128)(2,1)S(1)}, bf16[768,256]{1,0:T(8,128)(2,1)S(1)}, u32[]{:S(2)}, u32[]{:S(2)}) %collective-permute-start.14) | collective-permute-done | bytes 393248 | tf_op jit(solution)/shard_map/ppermute | solution.py:374
  101.6 3.2 %collective-permute-start.18 = (bf16[3072,256]{1,0:T(8,128)(2,1)S(1)}, bf16[3072,256]{1,0:T(8,128)(2,1)S(1)}, u32[]{:S(2)}, u32[]{:S(2)}) collective-permute-start(bf16[3072,256]{1,0:T(8,128)(2,1)S(1)} %bitcast.17), channel_id=1, source_target_pairs={{0,3},{1,0},{2,1},{3,2},{4,7},{5,4},{6,5},{7,6},{8,11},{9,8},{10,9... | collective-permute-start | bytes 4718600 | tf_op jit(solution)/shard_map/ppermute | solution.py:374
  106.5 3.6 %collective-permute-done.19.refs_6_ = f32[64,512]{1,0:T(8,128)S(1)} collective-permute-done((f32[64,512]{1,0:T(8,128)S(1)}, f32[64,512]{1,0:T(8,128)S(1)}, u32[]{:S(2)}, u32[]{:S(2)}) %collective-permute-start.19) | collective-permute-done | bytes 131104 | tf_op jit(solution)/shard_map/ppermute | solution.py:68
  112.8 3.2 %collective-permute-done.21.refs_8_ = f32[64,512]{1,0:T(8,128)S(1)} collective-permute-done((f32[64,512]{1,0:T(8,128)S(1)}, f32[64,512]{1,0:T(8,128)S(1)}, u32[]{:S(2)}, u32[]{:S(2)}) %collective-permute-start.21) | collective-permute-done | bytes 131104 | tf_op jit(solution)/shard_map/ppermute | solution.py:68
  118.0 22.1 %collective-permute-done.17.refs_1_ = bf16[3072,256]{1,0:T(8,128)(2,1)S(1)} collective-permute-done((bf16[3072,256]{1,0:T(8,128)(2,1)S(1)}, bf16[3072,256]{1,0:T(8,128)(2,1)S(1)}, u32[]{:S(2)}, u32[]{:S(2)}) %collective-permute-start.17) | collective-permute-done | bytes 1572896 | tf_op jit(solution)/shard_map/ppermute | solution.py:374
  141.3 5.9 %shard_map.137 = (f32[6,128,512]{2,1,0:T(8,128)S(1)}, f32[6,128,512]{2,1,0:T(8,128)S(1)}) custom-call(s32[6]{0:T(128)S(1)} %copy-done.6, bf16[3072,256]{1,0:T(8,128)(2,1)S(1)} %bitcast.19, bf16[3072,256]{1,0:T(8,128)(2,1)S(1)} %collective-permute-done.17.refs_1_, bf16[3072,256]{1,0:T(8,128)(2,1)S(1)} %collective-permute-done.18.refs_2_, ...), custom_call_target="tpu_custom_call" | custom-call | flops 2415919104 | bytes 4718592 | tf_op jit(solution)/shard_map/pallas_call | solution.py:295
  147.3 11.0 %shard_map.138 = f32[6,128,64]{2,1,0:T(8,128)S(1)} custom-call(s32[6]{0:T(128)S(1)} %copy-done.6, bf16[3072,256]{1,0:T(8,128)(2,1)S(1)} %collective-permute-done.16.refs_0_, bf16[6,2048,512]{2,1,0:T(8,128)(2,1)S(1)} %get-tuple-element.14.a.refs_3_.refs_1_, bf16[6,2048,512]{2,1,0:T(8,128)(2,1)S(1)} %copy-done.1, ...), custom_call_target="tpu_custom_call" | custom-call | flops 805306368 | bytes 1572864 | tf_op jit(solution)/shard_map/pallas_call | solution.py:342
  158.6 13.7 %all_to_all.10 = f32[16,1,3072]{2,1,0:T(1,128)S(1)} all-to-all(f32[16,1,3072]{2,1,0:T(1,128)S(1)} %reshape.23), channel_id=1, replica_groups=mesh['x'=4,'core'=2,'z'=4,'y'=4] {'z','y'}, dimensions={0} | all-to-all | bytes 393216 | tf_op jit(solution)/shard_map/all_to_all | solution.py:410
  174.9 3.5 %all-to-all-start.1 = ((f32[16,6,128]{2,1,0:T(8,128)}), f32[16,6,128]{2,1,0:T(8,128)S(1)}, u32[]{:S(2)}, u32[]{:S(2)}) async-start(f32[16,6,128]{2,1,0:T(8,128)} %broadcast_in_dim_broadcast_in_dim_broadcast_in_dim.2), calls=%async_computation.1 | async-start | bytes 131072 | tf_op jit(solution)/shard_map/all_to_all | solution.py:399
  178.4 7.5 %all-to-all-done.1 = f32[16,6,128]{2,1,0:T(8,128)S(1)} async-done(((f32[16,6,128]{2,1,0:T(8,128)}), f32[16,6,128]{2,1,0:T(8,128)S(1)}, u32[]{:S(2)}, u32[]{:S(2)}) %all-to-all-start.1) | async-done | bytes 49184 | tf_op jit(solution)/shard_map/all_to_all | solution.py:399
  (79 shorter events, 24.6 us)
Async XLA Ops:
  0.7 5.9 %collective-permute-start = (bf16[2,16,512]{2,1,0:T(8,128)(2,1)S(1)}, bf16[2,16,512]{2,1,0:T(8,128)(2,1)S(1)}, u32[]{:S(2)}, u32[]{:S(2)}) collective-permute-start(bf16[2,16,512]{2,1,0:T(8,128)(2,1)S(1)} %pad_maximum_fusion.1.refs_0_), channel_id=1, source_target_pairs={{0,16},{16,32},{32,48},{48,64},{64,80},{80,96},{96,112},{112,0},{1... | collective-permute-start | bytes 98312 | tf_op jit(solution)/shard_map/ppermute | solution.py:68
  0.8 5.9 %collective-permute-start.1 = (bf16[2,16,512]{2,1,0:T(8,128)(2,1)S(1)}, bf16[2,16,512]{2,1,0:T(8,128)(2,1)S(1)}, u32[]{:S(2)}, u32[]{:S(2)}) collective-permute-start(bf16[2,16,512]{2,1,0:T(8,128)(2,1)S(1)} %pad_maximum_fusion.1.refs_0_), channel_id=1, source_target_pairs={{0,32},{16,48},{32,64},{48,80},{64,96},{80,112},{96,0},{112,16},{1... | collective-permute-start | bytes 98312 | tf_op jit(solution)/shard_map/ppermute | solution.py:68
  1.2 14.7 %collective-permute-start.2 = (bf16[2,16,512]{2,1,0:T(8,128)(2,1)S(1)}, bf16[2,16,512]{2,1,0:T(8,128)(2,1)S(1)}, u32[]{:S(2)}, u32[]{:S(2)}) collective-permute-start(bf16[2,16,512]{2,1,0:T(8,128)(2,1)S(1)} %pad_maximum_fusion.1.refs_0_), channel_id=1, source_target_pairs={{0,48},{16,64},{32,80},{48,96},{64,112},{80,0},{96,16},{112,32},{1... | collective-permute-start | bytes 98312 | tf_op jit(solution)/shard_map/ppermute | solution.py:68
  3.6 12.3 %collective-permute-start.3 = (bf16[2,16,512]{2,1,0:T(8,128)(2,1)S(1)}, bf16[2,16,512]{2,1,0:T(8,128)(2,1)S(1)}, u32[]{:S(2)}, u32[]{:S(2)}) collective-permute-start(bf16[2,16,512]{2,1,0:T(8,128)(2,1)S(1)} %pad_maximum_fusion.1.refs_0_), channel_id=1, source_target_pairs={{0,64},{16,80},{32,96},{48,112},{64,0},{80,16},{96,32},{112,48},{1... | collective-permute-start | bytes 98312 | tf_op jit(solution)/shard_map/ppermute | solution.py:68
  4.7 11.2 %collective-permute-start.4 = (bf16[2,16,512]{2,1,0:T(8,128)(2,1)S(1)}, bf16[2,16,512]{2,1,0:T(8,128)(2,1)S(1)}, u32[]{:S(2)}, u32[]{:S(2)}) collective-permute-start(bf16[2,16,512]{2,1,0:T(8,128)(2,1)S(1)} %pad_maximum_fusion.1.refs_0_), channel_id=1, source_target_pairs={{0,80},{16,96},{32,112},{48,0},{64,16},{80,32},{96,48},{112,64},{1... | collective-permute-start | bytes 98312 | tf_op jit(solution)/shard_map/ppermute | solution.py:68
  6.7 9.3 %collective-permute-start.5 = (bf16[2,16,512]{2,1,0:T(8,128)(2,1)S(1)}, bf16[2,16,512]{2,1,0:T(8,128)(2,1)S(1)}, u32[]{:S(2)}, u32[]{:S(2)}) collective-permute-start(bf16[2,16,512]{2,1,0:T(8,128)(2,1)S(1)} %pad_maximum_fusion.1.refs_0_), channel_id=1, source_target_pairs={{0,96},{16,112},{32,0},{48,16},{64,32},{80,48},{96,64},{112,80},{1... | collective-permute-start | bytes 98312 | tf_op jit(solution)/shard_map/ppermute | solution.py:68
  6.7 9.3 %collective-permute-start.6 = (bf16[2,16,512]{2,1,0:T(8,128)(2,1)S(1)}, bf16[2,16,512]{2,1,0:T(8,128)(2,1)S(1)}, u32[]{:S(2)}, u32[]{:S(2)}) collective-permute-start(bf16[2,16,512]{2,1,0:T(8,128)(2,1)S(1)} %pad_maximum_fusion.1.refs_0_), channel_id=1, source_target_pairs={{0,112},{16,0},{32,16},{48,32},{64,48},{80,64},{96,80},{112,96},{1... | collective-permute-start | bytes 98312 | tf_op jit(solution)/shard_map/ppermute | solution.py:68
  27.0 38.2 %collective-permute-start.9 = (s16[3104,256]{1,0:T(8,128)(2,1)S(1)}, s16[3104,256]{1,0:T(8,128)(2,1)S(1)}, u32[]{:S(2)}, u32[]{:S(2)}) collective-permute-start(s16[3104,256]{1,0:T(8,128)(2,1)S(1)} %shard_map.132), channel_id=1, source_target_pairs={{0,3},{1,0},{2,1},{3,2},{4,7},{5,4},{6,5},{7,6},{8,11},{9,8},{10,9... | collective-permute-start | bytes 4767752 | tf_op jit(solution)/shard_map/ppermute | solution.py:374
  30.1 35.1 %collective-permute-start.8 = (s16[3104,256]{1,0:T(8,128)(2,1)S(1)}, s16[3104,256]{1,0:T(8,128)(2,1)S(1)}, u32[]{:S(2)}, u32[]{:S(2)}) collective-permute-start(s16[3104,256]{1,0:T(8,128)(2,1)S(1)} %shard_map.131), channel_id=1, source_target_pairs={{0,2},{1,3},{2,0},{3,1},{4,6},{5,7},{6,4},{7,5},{8,10},{9,11},{10,... | collective-permute-start | bytes 4767752 | tf_op jit(solution)/shard_map/ppermute | solution.py:374
  30.7 38.5 %collective-permute-start.7 = (s16[3104,256]{1,0:T(8,128)(2,1)S(1)}, s16[3104,256]{1,0:T(8,128)(2,1)S(1)}, u32[]{:S(2)}, u32[]{:S(2)}) collective-permute-start(s16[3104,256]{1,0:T(8,128)(2,1)S(1)} %shard_map.130), channel_id=1, source_target_pairs={{0,1},{1,2},{2,3},{3,0},{4,5},{5,6},{6,7},{7,4},{8,9},{9,10},{10,1... | collective-permute-start | bytes 4767752 | tf_op jit(solution)/shard_map/ppermute | solution.py:374
  70.0 9.9 %collective-permute-start.11 = (s16[800,256]{1,0:T(8,128)(2,1)S(1)}, s16[800,256]{1,0:T(8,128)(2,1)S(1)}, u32[]{:S(2)}, u32[]{:S(2)}) collective-permute-start(s16[800,256]{1,0:T(8,128)(2,1)S(1)} %shard_map.134), channel_id=1, source_target_pairs={{0,8},{1,9},{2,10},{3,11},{4,12},{5,13},{6,14},{7,15},{8,0},{9,1},... | collective-permute-start | bytes 1228808 | tf_op jit(solution)/shard_map/ppermute | solution.py:374
  76.3 9.2 %collective-permute-start.10 = (s16[800,256]{1,0:T(8,128)(2,1)S(1)}, s16[800,256]{1,0:T(8,128)(2,1)S(1)}, u32[]{:S(2)}, u32[]{:S(2)}) collective-permute-start(s16[800,256]{1,0:T(8,128)(2,1)S(1)} %get-tuple-element.18), channel_id=1, source_target_pairs={{0,4},{1,5},{2,6},{3,7},{4,8},{5,9},{6,10},{7,11},{8,12},{9,13},{1... | collective-permute-start | bytes 1228808 | tf_op jit(solution)/shard_map/ppermute | solution.py:374
  77.4 8.1 %collective-permute-start.12 = (s16[800,256]{1,0:T(8,128)(2,1)S(1)}, s16[800,256]{1,0:T(8,128)(2,1)S(1)}, u32[]{:S(2)}, u32[]{:S(2)}) collective-permute-start(s16[800,256]{1,0:T(8,128)(2,1)S(1)} %get-tuple-element.19), channel_id=1, source_target_pairs={{0,12},{1,13},{2,14},{3,15},{4,0},{5,1},{6,2},{7,3},{8,4},{9,5},{1... | collective-permute-start | bytes 1228808 | tf_op jit(solution)/shard_map/ppermute | solution.py:374
  86.0 9.1 %collective-permute-start.13 = (bf16[768,256]{1,0:T(8,128)(2,1)S(1)}, bf16[768,256]{1,0:T(8,128)(2,1)S(1)}, u32[]{:S(2)}, u32[]{:S(2)}) collective-permute-start(bf16[768,256]{1,0:T(8,128)(2,1)S(1)} %shard_map.135.r0), channel_id=1, source_target_pairs={{0,4},{1,5},{2,6},{3,7},{4,8},{5,9},{6,10},{7,11},{8,12},{9,13},{1... | collective-permute-start | bytes 1179656 | tf_op jit(solution)/shard_map/ppermute | solution.py:374
  86.9 14.5 %collective-permute-start.14 = (bf16[768,256]{1,0:T(8,128)(2,1)S(1)}, bf16[768,256]{1,0:T(8,128)(2,1)S(1)}, u32[]{:S(2)}, u32[]{:S(2)}) collective-permute-start(bf16[768,256]{1,0:T(8,128)(2,1)S(1)} %shard_map.135.r0), channel_id=1, source_target_pairs={{0,8},{1,9},{2,10},{3,11},{4,12},{5,13},{6,14},{7,15},{8,0},{9,1},... | collective-permute-start | bytes 1179656 | tf_op jit(solution)/shard_map/ppermute | solution.py:374
  90.8 10.6 %collective-permute-start.15 = (bf16[768,256]{1,0:T(8,128)(2,1)S(1)}, bf16[768,256]{1,0:T(8,128)(2,1)S(1)}, u32[]{:S(2)}, u32[]{:S(2)}) collective-permute-start(bf16[768,256]{1,0:T(8,128)(2,1)S(1)} %shard_map.135.r0), channel_id=1, source_target_pairs={{0,12},{1,13},{2,14},{3,15},{4,0},{5,1},{6,2},{7,3},{8,4},{9,5},{1... | collective-permute-start | bytes 1179656 | tf_op jit(solution)/shard_map/ppermute | solution.py:374
  101.5 38.5 %collective-permute-start.17 = (bf16[3072,256]{1,0:T(8,128)(2,1)S(1)}, bf16[3072,256]{1,0:T(8,128)(2,1)S(1)}, u32[]{:S(2)}, u32[]{:S(2)}) collective-permute-start(bf16[3072,256]{1,0:T(8,128)(2,1)S(1)} %bitcast.16), channel_id=1, source_target_pairs={{0,1},{1,2},{2,3},{3,0},{4,5},{5,6},{6,7},{7,4},{8,9},{9,10},{10,1... | collective-permute-start | bytes 4718600 | tf_op jit(solution)/shard_map/ppermute | solution.py:374
  101.6 39.7 %collective-permute-start.18 = (bf16[3072,256]{1,0:T(8,128)(2,1)S(1)}, bf16[3072,256]{1,0:T(8,128)(2,1)S(1)}, u32[]{:S(2)}, u32[]{:S(2)}) collective-permute-start(bf16[3072,256]{1,0:T(8,128)(2,1)S(1)} %bitcast.17), channel_id=1, source_target_pairs={{0,3},{1,0},{2,1},{3,2},{4,7},{5,4},{6,5},{7,6},{8,11},{9,8},{10,9... | collective-permute-start | bytes 4718600 | tf_op jit(solution)/shard_map/ppermute | solution.py:374
  104.8 42.4 %collective-permute-start.16 = (bf16[3072,256]{1,0:T(8,128)(2,1)S(1)}, bf16[3072,256]{1,0:T(8,128)(2,1)S(1)}, u32[]{:S(2)}, u32[]{:S(2)}) collective-permute-start(bf16[3072,256]{1,0:T(8,128)(2,1)S(1)} %bitcast.18), channel_id=1, source_target_pairs={{0,2},{1,3},{2,0},{3,1},{4,6},{5,7},{6,4},{7,5},{8,10},{9,11},{10,... | collective-permute-start | bytes 4718600 | tf_op jit(solution)/shard_map/ppermute | solution.py:374
  104.8 6.3 %collective-permute-start.20 = (f32[64,512]{1,0:T(8,128)S(1)}, f32[64,512]{1,0:T(8,128)S(1)}, u32[]{:S(2)}, u32[]{:S(2)}) collective-permute-start(f32[64,512]{1,0:T(8,128)S(1)} %pad_maximum_fusion.refs_5_), channel_id=1, source_target_pairs={{0,32},{16,48},{32,64},{48,80},{64,96},{80,112},{96,0},{112,16},{1... | collective-permute-start | bytes 393224 | tf_op jit(solution)/shard_map/ppermute | solution.py:68
  111.2 36.0 %collective-permute-start.22 = (f32[64,512]{1,0:T(8,128)S(1)}, f32[64,512]{1,0:T(8,128)S(1)}, u32[]{:S(2)}, u32[]{:S(2)}) collective-permute-start(f32[64,512]{1,0:T(8,128)S(1)} %pad_maximum_fusion.refs_5_), channel_id=1, source_target_pairs={{0,64},{16,80},{32,96},{48,112},{64,0},{80,16},{96,32},{112,48},{1... | collective-permute-start | bytes 393224 | tf_op jit(solution)/shard_map/ppermute | solution.py:68
  116.0 31.2 %collective-permute-start.23 = (f32[64,512]{1,0:T(8,128)S(1)}, f32[64,512]{1,0:T(8,128)S(1)}, u32[]{:S(2)}, u32[]{:S(2)}) collective-permute-start(f32[64,512]{1,0:T(8,128)S(1)} %pad_maximum_fusion.refs_5_), channel_id=1, source_target_pairs={{0,80},{16,96},{32,112},{48,0},{64,16},{80,32},{96,48},{112,64},{1... | collective-permute-start | bytes 393224 | tf_op jit(solution)/shard_map/ppermute | solution.py:68
  140.1 7.1 %collective-permute-start.24 = (f32[64,512]{1,0:T(8,128)S(1)}, f32[64,512]{1,0:T(8,128)S(1)}, u32[]{:S(2)}, u32[]{:S(2)}) collective-permute-start(f32[64,512]{1,0:T(8,128)S(1)} %pad_maximum_fusion.refs_5_), channel_id=1, source_target_pairs={{0,96},{16,112},{32,0},{48,16},{64,32},{80,48},{96,64},{112,80},{1... | collective-permute-start | bytes 393224 | tf_op jit(solution)/shard_map/ppermute | solution.py:68
  174.9 11.1 %all-to-all-start.1 = ((f32[16,6,128]{2,1,0:T(8,128)}), f32[16,6,128]{2,1,0:T(8,128)S(1)}, u32[]{:S(2)}, u32[]{:S(2)}) async-start(f32[16,6,128]{2,1,0:T(8,128)} %broadcast_in_dim_broadcast_in_dim_broadcast_in_dim.2), calls=%async_computation.1 | async-start | bytes 131072 | tf_op jit(solution)/shard_map/all_to_all | solution.py:399
  (14 other events, 336.8 us)
